TPU v7x, 128 devices: a whole 4x4x4 slice. The times are simulated.
128 devices in a mesh: facet: 8 (over x_lo, y), bl: 8 (over z, core), chan: 2 (over x_hi).
Axes of the slice: x: 4 (x_hi: 2, x_lo: 2; x = x_hi * 2 + x_lo), y: 4, z: 4, core: 2. Of those that a mesh axis runs over, the one named last changes fastest.
Arguments:
- visibilities: bfloat16 [512, 8, 2, 128], P(('facet', 'bl'), 'chan'), may hold values from -6 to 6
- coords: bfloat16 [512, 2, 128], P(('facet', 'bl')), may hold values from 4 to 124
- plane_index: int32 [512], P(('facet', 'bl')), may hold values from 0 to 63, as said below
- block_group: int32 [512, 1], P(('facet', 'bl')), may hold values from 0 to 7, as said below
- offsets: int32 [8, 8, 2], replicated, may hold values from 0 to 7
- facet_centre: float32 [8, 2], replicated, may hold values from -8 to 8
- tables: bfloat16 [64, 2, 128, 2, 128], P(('facet', 'bl')), may hold values from -0.5 to 0.5
- antenna_gain: float32 [8, 2, 128], P('bl'), may hold values from 0.1 to 1.9
Outputs:
- subgrids: float32 [8, 8, 128, 2, 128], P('facet', 'bl', 'chan')
Inputs may be any that keep to these rules, and one draw needn't show every extreme that they name: `block_group`: among the 8 blocks of one device at most 2 name the same baseline group, and on every device some group is named by exactly 2 of them. `plane_index`: A block whose baseline group is g names a w-plane p with p modulo 8 equal to g or to (g + 7) modulo 8.
All inputs are finite; a program needn't handle non-finite values.
Results may differ from a plain program's by a relative error of at most 0.0054.
Values may be sent and summed in bfloat16 or wider, within the bound.
A program may use at most 64 MiB of HBM per device.

v0:
```python
import math

import jax
import jax.numpy as jnp
from jax import lax
from jax.sharding import PartitionSpec as P

SU = 128
CH = 8


kernel_spread = 1.5


def channel_scale(count, first):
    index = (first + jnp.arange(count, dtype=jnp.int32)).astype(jnp.float32)
    return 1.0 + 0.01 * (index - 0.5 * (CH - 1))


def gather_whole(tables):
    whole_table = lax.all_gather(tables, ("facet", "bl"), axis=0, tiled=True)
    return whole_table.reshape(whole_table.shape[0], -1)


def block_grids(samples, place, planes, shifts, centre, flat_table, scale):
    count = samples.shape[0]
    chans = samples.shape[1]
    rows = samples.shape[3]
    planes_total = flat_table.shape[0]
    picks = (planes[:, None] == jnp.arange(planes_total, dtype=jnp.int32)[None, :]).astype(
        jnp.bfloat16
    )
    kernels = jnp.dot(picks, flat_table, preferred_element_type=jnp.float32).astype(jnp.bfloat16)
    kernels = kernels.reshape(count, 2, SU, 2 * SU)
    cells = jnp.arange(SU, dtype=jnp.int32).astype(jnp.float32)
    along_u = place[:, 0].astype(jnp.float32)
    along_v = place[:, 1].astype(jnp.float32)

    def profile(position, offset):
        spot = scale[None, :, None] * position[:, None, :] - offset[:, None, None]
        apart = spot[:, :, :, None] - cells
        return (
            jnp.exp(-apart * apart / (2.0 * kernel_spread * kernel_spread))
            .astype(jnp.bfloat16)
            .reshape(count, chans * rows, SU)
        )

    spread_u = jnp.einsum(
        "bsj,bjk->bsk",
        profile(along_u, shifts[:, 0]),
        kernels[:, 0],
        preferred_element_type=jnp.float32,
    )
    spread_v = jnp.einsum(
        "bsj,bjk->bsk",
        profile(along_v, shifts[:, 1]),
        kernels[:, 1],
        preferred_element_type=jnp.float32,
    ).astype(jnp.bfloat16)
    phase = (
        2.0
        * math.pi
        / SU
        * (scale[None, :, None] * (along_u * centre[0] + along_v * centre[1])[:, None, :])
    )
    phase = phase.reshape(count, chans * rows, 1)
    real_part = samples[:, :, 0].astype(jnp.float32).reshape(count, chans * rows, 1)
    imag_part = samples[:, :, 1].astype(jnp.float32).reshape(count, chans * rows, 1)
    cosine = jnp.cos(phase)
    sine = jnp.sin(phase)
    turned_real = real_part * cosine - imag_part * sine
    turned_imag = real_part * sine + imag_part * cosine
    weighted_real = spread_u[:, :, :SU] * turned_real - spread_u[:, :, SU:] * turned_imag
    weighted_imag = spread_u[:, :, :SU] * turned_imag + spread_u[:, :, SU:] * turned_real
    weighted = jnp.concatenate([weighted_real, weighted_imag], axis=2).astype(jnp.bfloat16)
    product = jnp.einsum("bsj,bsk->bjk", weighted, spread_v, preferred_element_type=jnp.float32)
    grid_real = product[:, :SU, :SU] - product[:, SU:, SU:]
    grid_imag = product[:, :SU, SU:] + product[:, SU:, :SU]
    return jnp.stack([grid_real, grid_imag], axis=2)


def fold_groups(total, arrays, grid_fn):
    count = arrays[0].shape[0]
    step_size = count
    while step_size > 16 and step_size % 2 == 0:
        step_size = step_size // 2
    parts = count // step_size
    shaped = tuple([item.reshape((parts, step_size) + item.shape[1:]) for item in arrays])

    def one_group(carry, group_items):
        return (carry + grid_fn(group_items), None)

    result, _ = lax.scan(one_group, total, shaped)
    return result


def body(
    visibilities, coords, plane_index, block_group, offsets, facet_centre, tables, antenna_gain
):
    facet_count = lax.axis_size("facet")
    group_count = lax.axis_size("bl")
    chan_count = lax.axis_size("chan")
    held = visibilities.shape[0]
    chans = visibilities.shape[1]
    facet_id = lax.axis_index("facet")
    group_id = lax.axis_index("bl")
    scale = channel_scale(chans, lax.axis_index("chan") * chans)
    offsets_here = lax.dynamic_index_in_dim(offsets, facet_id, 0, keepdims=False).astype(
        jnp.float32
    )
    centre = lax.dynamic_index_in_dim(facet_centre, facet_id, 0, keepdims=False)
    rows_out = SU // chan_count
    norm = SU / math.sqrt(visibilities.shape[3] * held * facet_count * CH)
    flat_table = gather_whole(tables)
    capacity = max(2, 2 * held // group_count)
    slots = group_count * capacity
    labels = block_group[:, 0]
    positions = jnp.arange(held, dtype=jnp.int32)
    earlier = positions[:, None] > positions[None, :]
    matching = labels[:, None] == labels[None, :]
    ranking = jnp.sum((earlier & matching).astype(jnp.int32), axis=1)
    target = labels * capacity + ranking
    hits = (target[None, :] == jnp.arange(slots, dtype=jnp.int32)[:, None]).astype(jnp.int32)
    source = jnp.sum(hits * positions[None, :], axis=1)
    filled = jnp.sum(hits, axis=1)
    samples_out = (
        jnp.take(visibilities, source, axis=0) * filled.astype(jnp.bfloat16)[:, None, None, None]
    )
    place_out = jnp.take(coords, source, axis=0)
    planes_out = jnp.where(filled > 0, jnp.take(plane_index, source), -1).astype(jnp.bfloat16)
    samples_in, place_in, planes_in = (
        lax.all_to_all(samples_out, "bl", split_axis=0, concat_axis=0, tiled=True),
        lax.all_to_all(place_out, "bl", split_axis=0, concat_axis=0, tiled=True),
        lax.all_to_all(planes_out, "bl", split_axis=0, concat_axis=0, tiled=True),
    )
    own_shift = lax.dynamic_index_in_dim(offsets_here, group_id, 0, keepdims=False)

    def slot_grid(items):
        piece_samples, piece_place, piece_planes = items
        count = piece_samples.shape[0]
        shifts = jnp.broadcast_to(own_shift[None, :], (count, 2))
        grids = block_grids(
            piece_samples,
            piece_place,
            piece_planes.astype(jnp.int32),
            shifts,
            centre,
            flat_table,
            scale,
        )
        return jnp.sum(grids, axis=0)

    empty = jnp.zeros((SU, 2, SU), jnp.float32)
    raw = fold_groups(
        empty,
        (
            lax.all_gather(samples_in, "facet", axis=0, tiled=True),
            lax.all_gather(place_in, "facet", axis=0, tiled=True),
            lax.all_gather(planes_in, "facet", axis=0, tiled=True),
        ),
        slot_grid,
    )
    rows_sum = lax.psum_scatter(raw, "chan", scatter_dimension=0, tiled=True)
    row_first = lax.axis_index("chan") * rows_out
    gain_u = lax.dynamic_slice_in_dim(antenna_gain[0, 0], row_first, rows_out)
    gain_v = antenna_gain[0, 1]
    gains = gain_u[:, None, None] * gain_v[None, None, :]
    result = rows_sum * gains * norm
    return result.reshape(1, 1, rows_out, 2, SU)


def solution(mesh):
    in_specs = (
        P(("facet", "bl"), "chan", None, None),
        P(("facet", "bl"), None, None),
        P(("facet", "bl")),
        P(("facet", "bl"), None),
        P(),
        P(),
        P(("facet", "bl"), None, None, None, None),
        P("bl", None, None),
    )
    out_specs = P("facet", "bl", "chan", None, None)
    return jax.shard_map(body, mesh=mesh, in_specs=in_specs, out_specs=out_specs, check_vma=False)
```

profile of v0, /device:TPU:0, one launch (start us, length us, event | category | flops | bytes accessed | tf_op | source)
XLA Modules:
  0.0 368.9 jit_solution(10373531865495988063)
XLA Ops:
  12.4 5.4 %all-to-all-start.1 = ((bf16[8,2,1]{1,2,0:T(2,128)(2,1)}), bf16[8,2,1]{1,2,0:T(2,128)(2,1)S(1)}, u32[]{:S(2)}, u32[]{:S(2)}) async-start(bf16[8,2,1]{1,2,0:T(2,128)(2,1)} %copy.59), calls=%async_computation.1 | async-start | bytes 8192 | tf_op jit(solution)/shard_map/all_to_all | solution.py:134
  23.0 4.3 %all-to-all-start = ((bf16[16,2,128]{2,1,0:T(2,128)(2,1)}), bf16[16,2,128]{2,1,0:T(2,128)(2,1)S(1)}, u32[]{:S(2)}, u32[]{:S(2)}) async-start(bf16[16,2,128]{2,1,0:T(2,128)(2,1)} %broadcast_select_fusion.1), calls=%async_computation | async-start | bytes 16384 | tf_op jit(solution)/shard_map/all_to_all | solution.py:133
  32.8 19.9 %all-reduce = bf16[128]{0:T(256)(128)(2,1)S(1)} all-reduce(bf16[128]{0:T(256)(128)(2,1)S(1)} %dynamic-update-slice), channel_id=1, replica_groups=mesh['facet'=8,'bl'=8,'chan'=2] {'facet'}, use_global_device_ids=true, to_apply=%add | all-reduce | flops 128 | bytes 512
  52.8 4.8 %all-to-all-start.2 = ((bf16[16,4,2,128]{3,2,1,0:T(2,128)(2,1)}), bf16[16,4,2,128]{3,2,1,0:T(2,128)(2,1)S(1)}, u32[]{:S(2)}, u32[]{:S(2)}) async-start(bf16[16,4,2,128]{3,2,1,0:T(2,128)(2,1)} %fusion.48), calls=%async_computation.2 | async-start | bytes 65536 | tf_op jit(solution)/shard_map/all_to_all | solution.py:132
  57.6 28.2 %all_gather.12 = bf16[128,2,128]{2,1,0:T(2,128)(2,1)S(1)} all-gather(bf16[16,2,128]{2,1,0:T(2,128)(2,1)S(1)} %all-to-all-done), channel_id=1, replica_groups=mesh['facet'=8,'bl'=8,'chan'=2] {'facet'}, dimensions={0}, use_global_device_ids=true | all-gather | bytes 73728 | tf_op jit(solution)/shard_map/all_gather | solution.py:158
  85.8 28.6 %all_gather.15 = bf16[128,4,2,128]{3,1,2,0:T(4,128)(2,1)S(1)} all-gather(bf16[16,4,2,128]{3,1,2,0:T(4,128)(2,1)S(1)} %copy.62), channel_id=1, replica_groups=mesh['facet'=8,'bl'=8,'chan'=2] {'facet'}, dimensions={0}, use_global_device_ids=true | all-gather | bytes 294912 | tf_op jit(solution)/shard_map/all_gather | solution.py:157
  114.4 9.5 %all-gather.2.cloned.1.call-done = bf16[64,2,128,2,128]{4,2,3,1,0:T(8,128)(2,1)} async-done(((bf16[1,2,128,2,128]{4,2,3,1,0:T(8,128)(2,1)}), bf16[64,2,128,2,128]{4,2,3,1,0:T(8,128)(2,1)}) %all-gather.2.cloned.1.call-update) | async-done | bytes 8388624 | tf_op jit(solution)/shard_map/all_gather | solution.py:21
  123.9 16.3 %copy.61 = bf16[64,2,128,2,128]{4,3,2,1,0:T(2,128)(2,1)} copy(bf16[64,2,128,2,128]{4,2,3,1,0:T(8,128)(2,1)} %all-gather.2.cloned.1.call-done) | data formatting | bytes 16777216 | tf_op jit(solution)/shard_map/all_gather | solution.py:21
  140.2 11.3 %reshape.289 = bf16[64,65536]{1,0:T(8,128)(2,1)} reshape(bf16[64,2,128,2,128]{4,3,2,1,0:T(2,128)(2,1)} %copy.61) | data formatting | bytes 16777216 | tf_op jit(solution)/shard_map/reshape | solution.py:22
  151.5 179.9 %while.11 = (s32[]{:T(128)}, f32[128,2,128]{2,0,1:T(8,128)S(1)}, bf16[8,16,2,128]{3,2,1,0:T(2,128)(2,1)S(1)}, f32[2]{0:T(128)S(1)}, bf16[8,16]{1,0:T(8,128)(2,1)...) while((s32[]{:T(128)}, f32[128,2,128]{2,0,1:T(8,128)S(1)}, ...), condition=%wide.region_5.6_spmd.clone, body=%wide.region_3.5_spmd.clone.sunk | while | flops 2313845760 | bytes 55842676 | solution.py:93
  154.9 4.6 %convolution_convert_fusion.2 = bf16[16,65536]{1,0:T(8,128)(2,1)S(1)} fusion(bf16[64,65536]{1,0:T(8,128)(2,1)} %get-tuple-element.294, s32[16]{0:T(128)S(1)} %fusion.78), kind=kOutput, calls=%fused_computation.4.clone.1 | convolution fusion | flops 135267328 | bytes 10485824 | tf_op jit(solution)/shard_map/while/body/eval_jaxpr/dot_general | solution.py:33
  162.1 3.7 subtract_convert_fusion.2
  165.8 5.5 %fusion.80 = f32[16,256,256]{2,1,0:T(8,128)} fusion(bf16[16,512,128]{1,2,0:T(8,128)(2,1)} %get-tuple-element.262, bf16[16,512,128]{1,2,0:T(8,128)(2,1)} %get-tuple-element.263, f32[16,512]{1,0:T(8,128)S(1)} %get-tuple-element.264, f32[128]{0:T(128)S(1)} %iota_convert_fusion.2, bf16[16,2,128,256]{3,2,1,0:T(8,128)(2,1)S(1)} %bitcast.153), kind=kOutput, calls=%fused_computation.13.clone.1 | convolution fusion | flops 1626341376 | bytes 9470464 | tf_op jit(solution)/shard_map/while/body/eval_jaxpr/bsj,bsk->bjk/dot_general | solution.py:76
  177.4 4.6 %convolution_convert_fusion.2 = bf16[16,65536]{1,0:T(8,128)(2,1)S(1)} fusion(bf16[64,65536]{1,0:T(8,128)(2,1)} %get-tuple-element.294, s32[16]{0:T(128)S(1)} %fusion.78), kind=kOutput, calls=%fused_computation.4.clone.1 | convolution fusion | flops 135267328 | bytes 10485824 | tf_op jit(solution)/shard_map/while/body/eval_jaxpr/dot_general | solution.py:33
  184.6 3.7 subtract_convert_fusion.2
  188.3 5.5 %fusion.80 = f32[16,256,256]{2,1,0:T(8,128)} fusion(bf16[16,512,128]{1,2,0:T(8,128)(2,1)} %get-tuple-element.262, bf16[16,512,128]{1,2,0:T(8,128)(2,1)} %get-tuple-element.263, f32[16,512]{1,0:T(8,128)S(1)} %get-tuple-element.264, f32[128]{0:T(128)S(1)} %iota_convert_fusion.2, bf16[16,2,128,256]{3,2,1,0:T(8,128)(2,1)S(1)} %bitcast.153), kind=kOutput, calls=%fused_computation.13.clone.1 | convolution fusion | flops 1626341376 | bytes 9470464 | tf_op jit(solution)/shard_map/while/body/eval_jaxpr/bsj,bsk->bjk/dot_general | solution.py:76
  199.9 4.6 %convolution_convert_fusion.2 = bf16[16,65536]{1,0:T(8,128)(2,1)S(1)} fusion(bf16[64,65536]{1,0:T(8,128)(2,1)} %get-tuple-element.294, s32[16]{0:T(128)S(1)} %fusion.78), kind=kOutput, calls=%fused_computation.4.clone.1 | convolution fusion | flops 135267328 | bytes 10485824 | tf_op jit(solution)/shard_map/while/body/eval_jaxpr/dot_general | solution.py:33
  207.1 3.7 subtract_convert_fusion.2
  210.8 5.5 %fusion.80 = f32[16,256,256]{2,1,0:T(8,128)} fusion(bf16[16,512,128]{1,2,0:T(8,128)(2,1)} %get-tuple-element.262, bf16[16,512,128]{1,2,0:T(8,128)(2,1)} %get-tuple-element.263, f32[16,512]{1,0:T(8,128)S(1)} %get-tuple-element.264, f32[128]{0:T(128)S(1)} %iota_convert_fusion.2, bf16[16,2,128,256]{3,2,1,0:T(8,128)(2,1)S(1)} %bitcast.153), kind=kOutput, calls=%fused_computation.13.clone.1 | convolution fusion | flops 1626341376 | bytes 9470464 | tf_op jit(solution)/shard_map/while/body/eval_jaxpr/bsj,bsk->bjk/dot_general | solution.py:76
  222.4 4.6 %convolution_convert_fusion.2 = bf16[16,65536]{1,0:T(8,128)(2,1)S(1)} fusion(bf16[64,65536]{1,0:T(8,128)(2,1)} %get-tuple-element.294, s32[16]{0:T(128)S(1)} %fusion.78), kind=kOutput, calls=%fused_computation.4.clone.1 | convolution fusion | flops 135267328 | bytes 10485824 | tf_op jit(solution)/shard_map/while/body/eval_jaxpr/dot_general | solution.py:33
  233.3 5.5 %fusion.80 = f32[16,256,256]{2,1,0:T(8,128)} fusion(bf16[16,512,128]{1,2,0:T(8,128)(2,1)} %get-tuple-element.262, bf16[16,512,128]{1,2,0:T(8,128)(2,1)} %get-tuple-element.263, f32[16,512]{1,0:T(8,128)S(1)} %get-tuple-element.264, f32[128]{0:T(128)S(1)} %iota_convert_fusion.2, bf16[16,2,128,256]{3,2,1,0:T(8,128)(2,1)S(1)} %bitcast.153), kind=kOutput, calls=%fused_computation.13.clone.1 | convolution fusion | flops 1626341376 | bytes 9470464 | tf_op jit(solution)/shard_map/while/body/eval_jaxpr/bsj,bsk->bjk/dot_general | solution.py:76
  244.9 4.6 %convolution_convert_fusion.2 = bf16[16,65536]{1,0:T(8,128)(2,1)S(1)} fusion(bf16[64,65536]{1,0:T(8,128)(2,1)} %get-tuple-element.294, s32[16]{0:T(128)S(1)} %fusion.78), kind=kOutput, calls=%fused_computation.4.clone.1 | convolution fusion | flops 135267328 | bytes 10485824 | tf_op jit(solution)/shard_map/while/body/eval_jaxpr/dot_general | solution.py:33
  255.8 5.5 %fusion.80 = f32[16,256,256]{2,1,0:T(8,128)} fusion(bf16[16,512,128]{1,2,0:T(8,128)(2,1)} %get-tuple-element.262, bf16[16,512,128]{1,2,0:T(8,128)(2,1)} %get-tuple-element.263, f32[16,512]{1,0:T(8,128)S(1)} %get-tuple-element.264, f32[128]{0:T(128)S(1)} %iota_convert_fusion.2, bf16[16,2,128,256]{3,2,1,0:T(8,128)(2,1)S(1)} %bitcast.153), kind=kOutput, calls=%fused_computation.13.clone.1 | convolution fusion | flops 1626341376 | bytes 9470464 | tf_op jit(solution)/shard_map/while/body/eval_jaxpr/bsj,bsk->bjk/dot_general | solution.py:76
  267.4 4.6 %convolution_convert_fusion.2 = bf16[16,65536]{1,0:T(8,128)(2,1)S(1)} fusion(bf16[64,65536]{1,0:T(8,128)(2,1)} %get-tuple-element.294, s32[16]{0:T(128)S(1)} %fusion.78), kind=kOutput, calls=%fused_computation.4.clone.1 | convolution fusion | flops 135267328 | bytes 10485824 | tf_op jit(solution)/shard_map/while/body/eval_jaxpr/dot_general | solution.py:33
  274.6 3.7 subtract_convert_fusion.2
  278.2 5.5 %fusion.80 = f32[16,256,256]{2,1,0:T(8,128)} fusion(bf16[16,512,128]{1,2,0:T(8,128)(2,1)} %get-tuple-element.262, bf16[16,512,128]{1,2,0:T(8,128)(2,1)} %get-tuple-element.263, f32[16,512]{1,0:T(8,128)S(1)} %get-tuple-element.264, f32[128]{0:T(128)S(1)} %iota_convert_fusion.2, bf16[16,2,128,256]{3,2,1,0:T(8,128)(2,1)S(1)} %bitcast.153), kind=kOutput, calls=%fused_computation.13.clone.1 | convolution fusion | flops 1626341376 | bytes 9470464 | tf_op jit(solution)/shard_map/while/body/eval_jaxpr/bsj,bsk->bjk/dot_general | solution.py:76
  289.9 4.6 %convolution_convert_fusion.2 = bf16[16,65536]{1,0:T(8,128)(2,1)S(1)} fusion(bf16[64,65536]{1,0:T(8,128)(2,1)} %get-tuple-element.294, s32[16]{0:T(128)S(1)} %fusion.78), kind=kOutput, calls=%fused_computation.4.clone.1 | convolution fusion | flops 135267328 | bytes 10485824 | tf_op jit(solution)/shard_map/while/body/eval_jaxpr/dot_general | solution.py:33
  300.7 5.5 %fusion.80 = f32[16,256,256]{2,1,0:T(8,128)} fusion(bf16[16,512,128]{1,2,0:T(8,128)(2,1)} %get-tuple-element.262, bf16[16,512,128]{1,2,0:T(8,128)(2,1)} %get-tuple-element.263, f32[16,512]{1,0:T(8,128)S(1)} %get-tuple-element.264, f32[128]{0:T(128)S(1)} %iota_convert_fusion.2, bf16[16,2,128,256]{3,2,1,0:T(8,128)(2,1)S(1)} %bitcast.153), kind=kOutput, calls=%fused_computation.13.clone.1 | convolution fusion | flops 1626341376 | bytes 9470464 | tf_op jit(solution)/shard_map/while/body/eval_jaxpr/bsj,bsk->bjk/dot_general | solution.py:76
  312.4 4.6 %convolution_convert_fusion.2 = bf16[16,65536]{1,0:T(8,128)(2,1)S(1)} fusion(bf16[64,65536]{1,0:T(8,128)(2,1)} %get-tuple-element.294, s32[16]{0:T(128)S(1)} %fusion.78), kind=kOutput, calls=%fused_computation.4.clone.1 | convolution fusion | flops 135267328 | bytes 10485824 | tf_op jit(solution)/shard_map/while/body/eval_jaxpr/dot_general | solution.py:33
  319.6 3.7 subtract_convert_fusion.2
  323.2 5.5 %fusion.80 = f32[16,256,256]{2,1,0:T(8,128)} fusion(bf16[16,512,128]{1,2,0:T(8,128)(2,1)} %get-tuple-element.262, bf16[16,512,128]{1,2,0:T(8,128)(2,1)} %get-tuple-element.263, f32[16,512]{1,0:T(8,128)S(1)} %get-tuple-element.264, f32[128]{0:T(128)S(1)} %iota_convert_fusion.2, bf16[16,2,128,256]{3,2,1,0:T(8,128)(2,1)S(1)} %bitcast.153), kind=kOutput, calls=%fused_computation.13.clone.1 | convolution fusion | flops 1626341376 | bytes 9470464 | tf_op jit(solution)/shard_map/while/body/eval_jaxpr/bsj,bsk->bjk/dot_general | solution.py:76
  332.3 28.3 %all-reduce.4.cloned.1.call-done = f32[128,2,128]{2,1,0:T(2,128)} async-done(((f32[128,2,128]{2,1,0:T(2,128)}), f32[128,2,128]{2,1,0:T(2,128)}) %all-reduce.4.cloned.1.call-update) | async-done | bytes 131088
  (211 shorter events, 96.7 us)
Async XLA Ops:
  6.5 11.3 %copy-start = (bf16[8,4,2,128]{3,2,1,0:T(2,128)(2,1)S(1)}, bf16[8,4,2,128]{3,2,1,0:T(2,128)(2,1)}, u32[]{:S(2)}) copy-start(bf16[8,4,2,128]{3,2,1,0:T(2,128)(2,1)} %param.10) | copy-start | bytes 49156
  6.5 117.4 %all-gather.2.cloned.1.call-start = ((), (), s32[]{:S(2)}) async-start(), calls=%async_computation.3 | async-start | bytes 8519680 | tf_op jit(solution)/shard_map/all_gather | solution.py:21
  12.4 10.7 %all-to-all-start.1 = ((bf16[8,2,1]{1,2,0:T(2,128)(2,1)}), bf16[8,2,1]{1,2,0:T(2,128)(2,1)S(1)}, u32[]{:S(2)}, u32[]{:S(2)}) async-start(bf16[8,2,1]{1,2,0:T(2,128)(2,1)} %copy.59), calls=%async_computation.1 | async-start | bytes 8192 | tf_op jit(solution)/shard_map/all_to_all | solution.py:134
  23.0 29.7 %all-to-all-start = ((bf16[16,2,128]{2,1,0:T(2,128)(2,1)}), bf16[16,2,128]{2,1,0:T(2,128)(2,1)S(1)}, u32[]{:S(2)}, u32[]{:S(2)}) async-start(bf16[16,2,128]{2,1,0:T(2,128)(2,1)} %broadcast_select_fusion.1), calls=%async_computation | async-start | bytes 16384 | tf_op jit(solution)/shard_map/all_to_all | solution.py:133
  52.8 33.0 %all-to-all-start.2 = ((bf16[16,4,2,128]{3,2,1,0:T(2,128)(2,1)}), bf16[16,4,2,128]{3,2,1,0:T(2,128)(2,1)S(1)}, u32[]{:S(2)}, u32[]{:S(2)}) async-start(bf16[16,4,2,128]{3,2,1,0:T(2,128)(2,1)} %fusion.48), calls=%async_computation.2 | async-start | bytes 65536 | tf_op jit(solution)/shard_map/all_to_all | solution.py:132
  57.6 303.0 %all-reduce.4.cloned.1.call-start = ((), (), s32[]{:S(2)}) async-start(), calls=%async_computation.4 | async-start | bytes 262144
Sparse Core Ops, SparseCore 0:
  9.1 114.7 all-gather.1
  332.3 28.1 all-reduce.3
where the time goes:
time: 371 us; the launch traced here: 369 us
  matrix products  97.8 us (26%)
  other arithmetic  76.7 us (21%)
  blocking collectives  76.7 us (21%)
  local copies, waits for them, and re-layouts  48.9 us (13%)
  waiting for transfers between devices  38.3 us (10%)
  between operations  14.8 us (4%)
  starting transfers between devices  14.6 us (4%)
    dot_general x8, matrix products, block_grids(): jnp.einsum('bsj,bsk->bjk', weighted, spread_v, preferred_element_type=jnp...  44.2 us
    dot_general x8, matrix products, block_grids(): jnp.dot(picks, flat_table, preferred_element_type=jnp.float32)  37.1 us
    another operation x8, other arithmetic  29.4 us
    all_gather x1, blocking collectives, body(): lax.all_gather(samples_in, 'facet', axis=0, tiled=True)  28.6 us
    unnamed x3, waiting for transfers between devices  28.3 us
    all_gather x1, blocking collectives, body(): lax.all_gather(place_in, 'facet', axis=0, tiled=True)  28.2 us
    another operation x8, other arithmetic, block_grids(): return jnp.stack([grid_real, grid_imag], axis=2)  20.1 us
    unnamed x1, blocking collectives  19.9 us
  transfers between devices with their start and end apart: 5, of which 3 were waited for; matrix products, arithmetic and copies ran while one was open for 4% of the time, Pallas kernels for 0%

commit v1 on v0

v1 whole, which is shorter than its diff:
```python
import math

import jax
import jax.numpy as jnp
from jax import lax
from jax.experimental import pallas as pl
from jax.experimental.pallas import tpu as pltpu
from jax.sharding import PartitionSpec as P

SU = 128
CH = 8
SPREAD = 1.5
ROOT = math.sqrt(math.log2(math.e) / (2.0 * SPREAD * SPREAD))
MESH = pl.DeviceIdType.MESH
F32 = jnp.float32
BF16 = jnp.bfloat16
TILES = 11
STEP = 4


def route_kernel(
    pack_ref, group_ref, tab_ref, blocks_ref, tabs_ref,
    send, recv, stage, a_send, a_recv, b_send, b_recv, t_send, t_recv, own_sem,
):
    f = lax.axis_index("facet")
    g = lax.axis_index("bl")
    c = lax.axis_index("chan")
    before = lax.rem(g + 7, 8)
    after = lax.rem(g + 1, 8)

    barrier = pltpu.get_barrier_semaphore()
    for d in range(1, 8):
        pl.semaphore_signal(
            barrier, inc=1, device_id=(f, lax.rem(g + d, 8), c), device_id_type=MESH
        )
        pl.semaphore_signal(
            barrier, inc=1, device_id=(lax.rem(f + d, 8), g, c), device_id_type=MESH
        )
        pl.semaphore_signal(
            barrier, inc=1, device_id=(lax.rem(f + d, 8), before, c), device_id_type=MESH
        )

    labels = [group_ref[n, 0] for n in range(8)]

    def build(group, carry):
        zero = jnp.int32(0)
        i0, i1, n0, n1 = zero, zero, zero, zero
        for n in reversed(range(8)):
            match = labels[n] == group
            i1 = jnp.where(match, i0, i1)
            n1 = jnp.where(match, n0, n1)
            i0 = jnp.where(match, n, i0)
            n0 = jnp.where(match, 1, n0)
        one = pack_ref[i0].astype(F32) * n0.astype(F32)
        two = pack_ref[i1].astype(F32) * n1.astype(F32)
        send[group, 0] = jnp.concatenate([one[:8], two[:8]], axis=0).astype(BF16)
        send[group, 1] = jnp.concatenate([one[8:], two[8:]], axis=0).astype(BF16)
        return carry

    lax.fori_loop(0, 8, build, 0)
    pl.semaphore_wait(barrier, 21)

    def copy_a(d, peer):
        return pltpu.make_async_remote_copy(
            src_ref=send.at[peer], dst_ref=recv.at[g], send_sem=a_send.at[d],
            recv_sem=a_recv.at[g], device_id=(f, peer, c), device_id_type=MESH,
        )

    def copy_t(d, shift):
        facet = lax.rem(f + d, 8)
        return pltpu.make_async_remote_copy(
            src_ref=tab_ref, dst_ref=tabs_ref.at[f, shift], send_sem=t_send.at[shift, d],
            recv_sem=t_recv.at[shift, f], device_id=(facet, after if shift else g, c),
            device_id_type=MESH,
        )

    def copy_b(d):
        return pltpu.make_async_remote_copy(
            src_ref=stage, dst_ref=blocks_ref.at[f], send_sem=b_send.at[d],
            recv_sem=b_recv.at[f], device_id=(lax.rem(f + d, 8), g, c), device_id_type=MESH,
        )

    for d in range(1, 8):
        copy_a(d, lax.rem(g + d, 8)).start()
    for d in range(8):
        for shift in (0, 1):
            if d or shift:
                copy_t(d, shift).start()
    own_tab = pltpu.make_async_copy(tab_ref, tabs_ref.at[f, 0], own_sem.at[0])
    own_tab.start()
    recv[g] = send[g]
    for d in range(1, 8):
        peer = lax.rem(g + d, 8)
        pltpu.make_async_remote_copy(
            src_ref=send.at[peer], dst_ref=recv.at[peer], send_sem=a_send.at[d],
            recv_sem=a_recv.at[peer], device_id=(f, peer, c), device_id_type=MESH,
        ).wait_recv()

    rows = lax.broadcasted_iota(jnp.int32, (16, SU), 0)
    extra = [jnp.zeros((16, SU), F32) for _ in range(3)]
    for b in range(8):
        stage[b] = recv[b, 0]
        misc = recv[b, 1].astype(F32)
        for k in range(2):
            here = rows == 2 * b + k
            for e in range(3):
                line = 8 * k + e
                extra[e] = jnp.where(here, misc[line : line + 1], extra[e])
    for e in range(3):
        stage[8 + e] = extra[e].astype(BF16)
    for d in range(1, 8):
        copy_b(d).start()
    own_blocks = pltpu.make_async_copy(stage, blocks_ref.at[f], own_sem.at[1])
    own_blocks.start()
    for d in range(1, 8):
        peer = lax.rem(f + d, 8)
        pltpu.make_async_remote_copy(
            src_ref=stage, dst_ref=blocks_ref.at[peer], send_sem=b_send.at[d],
            recv_sem=b_recv.at[peer], device_id=(peer, g, c), device_id_type=MESH,
        ).wait_recv()
    for d in range(8):
        peer = lax.rem(f + d, 8)
        for shift in (0, 1):
            if d or shift:
                pltpu.make_async_remote_copy(
                    src_ref=tab_ref, dst_ref=tabs_ref.at[peer, shift],
                    send_sem=t_send.at[shift, d], recv_sem=t_recv.at[shift, peer],
                    device_id=(peer, after if shift else g, c), device_id_type=MESH,
                ).wait_recv()
    own_tab.wait()
    own_blocks.wait()
    for d in range(1, 8):
        copy_a(d, lax.rem(g + d, 8)).wait_send()
        copy_b(d).wait_send()
    for d in range(8):
        for shift in (0, 1):
            if d or shift:
                copy_t(d, shift).wait_send()


def sine_of_turns(turns):
    part = turns - jnp.floor(turns + 0.5)
    part = jnp.maximum(jnp.minimum(part, 0.5 - part), -0.5 - part)
    angle = part * (2.0 * math.pi)
    square = angle * angle
    total = jnp.full_like(angle, -1.0 / math.factorial(11))
    for power in (9, 7, 5, 3, 1):
        sign = 1.0 if power % 4 == 1 else -1.0
        total = total * square + sign / math.factorial(power)
    return total * angle


def grid_kernel(
    blocks_ref, offsets_ref, centre_ref, tabs_hbm, keep_ref, give_ref,
    vis, line_u, line_v, order_v, order, turned, spots, planes, tabs, raw, sems,
):
    f = lax.axis_index("facet")
    g = lax.axis_index("bl")
    c = lax.axis_index("chan")
    fetch = pltpu.make_async_copy(tabs_hbm, tabs, sems.at[0])
    fetch.start()

    sub = lax.broadcasted_iota(jnp.int32, (SU, SU), 0)
    lane = lax.broadcasted_iota(jnp.int32, (SU, SU), 1)
    label = jnp.concatenate([blocks_ref[i, 10] for i in range(8)], axis=0)
    label = label.astype(F32).astype(jnp.int32) - 1
    number = (label >> 3) * 2 + jnp.where((label & 7) == g, 0, 1)
    number = jnp.where(label >= 0, number, 16).astype(F32)
    across = number.T
    ahead = (across < number) | ((across == number) & (lane < sub))
    place = jnp.sum(jnp.where(ahead, 1.0, 0.0), axis=1, keepdims=True)
    hit = place == lane.astype(F32)
    lines = [
        jnp.sum(jnp.where(hit, sub.astype(F32), 0.0), axis=0, keepdims=True),
        jnp.sum(jnp.where(hit, number, 0.0), axis=0, keepdims=True),
        jnp.sum(jnp.where(number < 16.0, 1.0, 0.0), axis=0, keepdims=True),
        jnp.zeros((5, SU), F32),
    ]
    order_v[...] = jnp.concatenate(lines, axis=0).astype(jnp.int32)
    orders = pltpu.make_async_copy(order_v, order, sems.at[1])
    orders.start()

    for i in range(8):
        line_u[16 * i : 16 * i + 16] = blocks_ref[i, 8].astype(F32)
        line_v[16 * i : 16 * i + 16] = blocks_ref[i, 9].astype(F32)
        for b in range(8):
            both = blocks_ref[i, b].astype(F32)
            vis[16 * i + 2 * b] = both[:8]
            vis[16 * i + 2 * b + 1] = both[8:]
    planes[...] = jnp.zeros_like(planes)
    orders.wait()
    steps = (order[2, 0] + STEP - 1) // STEP

    off_u = offsets_ref[f, g, 0].astype(F32)
    off_v = offsets_ref[f, g, 1].astype(F32)
    dir_l = centre_ref[f, 0]
    dir_m = centre_ref[f, 1]
    row = lax.broadcasted_iota(jnp.int32, (8, SU), 0)
    upper = row < 4
    channel = (c * 4 + (row & 3)).astype(F32)
    scale = 1.0 + 0.01 * (channel - 0.5 * (CH - 1))

    def prepare(step, carry):
        for q in range(STEP):
            at = step * STEP + q
            slot = order[0, at]
            u = line_u[pl.ds(slot, 1), :]
            v = line_v[pl.ds(slot, 1), :]
            along = jnp.where(upper, scale * u - off_u, scale * v - off_v)
            spots[at] = along * ROOT
            turns = (scale * (u * dir_l + v * dir_m)) * (1.0 / SU)
            turns = turns - jnp.floor(turns + 0.5)
            wave = sine_of_turns(turns + jnp.where(upper, 0.25, 0.0))
            data = vis[slot]
            straight = data * wave
            crossed = data * pltpu.roll(wave, 4, 0)
            turned[at] = jnp.where(
                upper, straight - pltpu.roll(straight, 4, 0), crossed + pltpu.roll(crossed, 4, 0)
            )
        return carry

    lax.fori_loop(0, steps, prepare, 0)

    cells = sub.astype(F32) * ROOT

    def profile(line):
        apart = line - cells
        return jnp.exp2(-(apart * apart)).astype(BF16)

    def gather(step, carry):
        for q in range(STEP):
            at = step * STEP + q
            along_u, real, imag = [], [], []
            for ch in range(4):
                along_u.append(profile(spots[at, ch : ch + 1, :]))
                along_v = profile(spots[at, 4 + ch : 5 + ch, :])
                real.append(along_v * turned[at, ch : ch + 1, :].astype(BF16))
                imag.append(along_v * turned[at, 4 + ch : 5 + ch, :].astype(BF16))
            left = jnp.concatenate(along_u, axis=1)
            right = jnp.concatenate(
                [jnp.concatenate(real, axis=1), jnp.concatenate(imag, axis=1)], axis=0
            )
            planes[order[1, at]] += lax.dot_general(
                left, right, (((1,), (1,)), ((), ())), preferred_element_type=F32
            )
        return carry

    lax.fori_loop(0, steps, gather, 0)
    fetch.wait()

    def turn(re, im):
        return jnp.concatenate(
            [jnp.concatenate([re, im], axis=1), jnp.concatenate([-im, re], axis=1)], axis=0
        )

    total = jnp.zeros((SU, 2 * SU), F32)
    for p in range(16):
        tab = tabs.at[p // 2, p % 2]
        part = jnp.dot(
            planes[p].astype(BF16), turn(tab[2], tab[3]), preferred_element_type=F32
        ).astype(BF16)
        total = total + jnp.dot(
            jnp.concatenate([tab[0], tab[1]], axis=1),
            turn(part[:, :SU], part[:, SU:]),
            preferred_element_type=F32,
        )
    raw[...] = total
    keep_ref[...] = raw[pl.ds(pl.multiple_of(c * 64, 64), 64), :]
    give_ref[...] = raw[pl.ds(pl.multiple_of((1 - c) * 64, 64), 64), :]


def body(
    visibilities, coords, plane_index, block_group, offsets, facet_centre, tables, antenna_gain
):
    held = visibilities.shape[0]
    norm = SU / math.sqrt(visibilities.shape[3] * held * 8 * CH)
    named = (plane_index + 1).astype(BF16)[:, None, None]
    pack = jnp.concatenate(
        [
            visibilities.transpose(0, 2, 1, 3).reshape(held, 8, SU),
            coords,
            jnp.broadcast_to(named, (held, 1, SU)),
            jnp.zeros((held, 5, SU), BF16),
        ],
        axis=1,
    )
    table = jnp.concatenate(
        [tables[0, 0].transpose(1, 2, 0), tables[0, 1].transpose(1, 0, 2)], axis=0
    )
    vmem = pl.BlockSpec(memory_space=pltpu.VMEM)
    smem = pl.BlockSpec(memory_space=pltpu.SMEM)
    hbm = pl.BlockSpec(memory_space=pl.ANY)
    dma = pltpu.SemaphoreType.DMA
    blocks, tabs = pl.pallas_call(
        route_kernel,
        out_shape=(
            jax.ShapeDtypeStruct((8, TILES, 16, SU), BF16),
            jax.ShapeDtypeStruct((8, 2, 4, SU, SU), BF16),
        ),
        in_specs=[vmem, smem, hbm],
        out_specs=(hbm, hbm),
        scratch_shapes=[
            pltpu.VMEM((8, 2, 16, SU), BF16),
            pltpu.VMEM((8, 2, 16, SU), BF16),
            pltpu.VMEM((TILES, 16, SU), BF16),
            dma((8,)), dma((8,)), dma((8,)), dma((8,)), dma((2, 8)), dma((2, 8)), dma((2,)),
        ],
        compiler_params=pltpu.CompilerParams(
            collective_id=0, has_side_effects=True, vmem_limit_bytes=16 * 2**20
        ),
        name="route",
    )(pack, block_group, table)
    half = jax.ShapeDtypeStruct((64, 2 * SU), F32)
    keep, give = pl.pallas_call(
        grid_kernel,
        out_shape=(half, half),
        in_specs=[vmem, smem, smem, hbm],
        out_specs=(vmem, vmem),
        scratch_shapes=[
            pltpu.VMEM((128, 8, SU), F32),
            pltpu.VMEM((128, SU), F32),
            pltpu.VMEM((128, SU), F32),
            pltpu.VMEM((8, SU), jnp.int32),
            pltpu.SMEM((8, SU), jnp.int32),
            pltpu.VMEM((128, 8, SU), F32),
            pltpu.VMEM((128, 8, SU), F32),
            pltpu.VMEM((17, SU, 2 * SU), F32),
            pltpu.VMEM((8, 2, 4, SU, SU), BF16),
            pltpu.VMEM((SU, 2 * SU), F32),
            dma((2,)),
        ],
        compiler_params=pltpu.CompilerParams(vmem_limit_bytes=32 * 2**20),
        name="grid",
    )(blocks, offsets, facet_centre, tabs)
    came = lax.ppermute(give, "chan", [(0, 1), (1, 0)])
    gain_u = lax.dynamic_slice_in_dim(antenna_gain[0, 0], lax.axis_index("chan") * 64, 64)
    gains = gain_u[:, None, None] * antenna_gain[0, 1][None, None, :] * norm
    result = (keep + came).reshape(64, 2, SU) * gains
    return result.reshape(1, 1, 64, 2, SU)


def solution(mesh):
    in_specs = (
        P(("facet", "bl"), "chan", None, None),
        P(("facet", "bl"), None, None),
        P(("facet", "bl")),
        P(("facet", "bl"), None),
        P(),
        P(),
        P(("facet", "bl"), None, None, None, None),
        P("bl", None, None),
    )
    out_specs = P("facet", "bl", "chan", None, None)
    return jax.shard_map(body, mesh=mesh, in_specs=in_specs, out_specs=out_specs, check_vma=False)
```

time: 371 us -> 68.7 us (0.19)
  matrix products: 97.8 us -> 0 us
  blocking collectives: 76.7 us -> 0 us
  other arithmetic: 76.7 us -> 2.19 us
  Pallas kernels: 0 us -> 55.6 us
  local copies, waits for them, and re-layouts: 48.9 us -> 4.4 us
  waiting for transfers between devices: 38.3 us -> 3.03 us
  between operations: 14.8 us -> 0.06 us
  starting transfers between devices: 14.6 us -> 2.66 us
    dot_general x24 -> x0, matrix products: 97.8 us -> none  [the longest x8 44.2 us: block_grids(): jnp.einsum('bsj,bsk->bjk', weighted, spread_v, preferred_element_type=jnp...]
    all_gather x2 -> x0, blocking collectives: 56.8 us -> none  [the longest x1 28.6 us: body(): lax.all_gather(samples_in, 'facet', axis=0, tiled=True)]
    pallas_call x0 -> x2, Pallas kernels: none -> 55.6 us  [the longest x1 42.4 us: body(): pl.pallas_call(route_kernel, out_shape=(jax.ShapeDtypeStruct((8, TILES, 1...]
    another operation x16 -> x0, other arithmetic: 49.5 us -> none
    unnamed x3 -> x0, waiting for transfers between devices: 28.3 us -> none
    unnamed x1 -> x0, blocking collectives: 19.9 us -> none
    all_gather x1 -> x0, local copies, waits for them, and re-layouts: 16.3 us -> none  [gather_whole(): whole_table = lax.all_gather(tables, ('facet', 'bl'), axis=0, tiled=True)]
    all_to_all x3 -> x0, starting transfers between devices: 14.5 us -> none  [the longest x1 5.4 us: body(): lax.all_to_all(planes_out, 'bl', split_axis=0, concat_axis=0, tiled=True)]
  transfers between devices with their start and end apart: 5 -> 1, of which waited for: 3 -> 1; matrix products, arithmetic and copies ran while one was open for 4% -> 0% of each run, Pallas kernels for 0% -> 0%
where the time goes in v1:
time: 68.7 us; the launch traced here: 68 us
  Pallas kernels  55.6 us (81%)
  local copies, waits for them, and re-layouts  4.4 us (6%)
  waiting for transfers between devices  3.03 us (4%)
  starting transfers between devices  2.66 us (4%)
  other arithmetic  2.19 us (3%)
    pallas_call x1, Pallas kernels, body(): pl.pallas_call(route_kernel, out_shape=(jax.ShapeDtypeStruct((8, TILES, 1...  42.4 us
    pallas_call x1, Pallas kernels, body(): pl.pallas_call(grid_kernel, out_shape=(half, half), in_specs=[vmem, smem,...  13.3 us
    ppermute x1, waiting for transfers between devices, body(): came = lax.ppermute(give, 'chan', [(0, 1), (1, 0)])  3.03 us
    ppermute x1, starting transfers between devices, body(): came = lax.ppermute(give, 'chan', [(0, 1), (1, 0)])  2.66 us
    unnamed x7, local copies, waits for them, and re-layouts  2.43 us
  transfers between devices with their start and end apart: 1, of which 1 were waited for; matrix products, arithmetic and copies ran while one was open for 0% of the time, Pallas kernels for 0%

profile of v1, /device:TPU:0, one launch (start us, length us, event | category | flops | bytes accessed | tf_op | source)
XLA Modules:
  0.0 68.0 jit_solution(6401617220155893264)
XLA Ops:
  0.0 0.0 copy-start
  0.0 1.0 %fusion = (bf16[1,1,128,2,128]{4,3,2,1,0:T(2,128)(2,1)S(1)}, bf16[1,1,128,2,128]{4,3,2,1,0:T(2,128)(2,1)S(1)}) fusion(bf16[1,2,128,2,128]{4,3,2,1,0:T(2,128)(2,1)} %param.14), kind=kLoop, calls=%fused_computation.8 | loop fusion | bytes 262144 | tf_op jit(solution)/shard_map/slice | solution.py:288
  1.0 0.1 copy.15
  1.1 0.7 %copy.9 = bf16[8,2,4,128]{3,2,1,0:T(4,128)(2,1)S(1)} copy(bf16[8,2,4,128]{3,1,2,0:T(2,128)(2,1)} %bitcast.17) | data formatting | bytes 32768 | tf_op jit(solution)/shard_map/transpose | solution.py:280
  1.9 0.7 add_convert_fusion
  2.5 0.7 %copy.12.group_ref = s32[8,1]{1,0:T(8,128)S(1)} copy(s32[8,1]{0,1:T(1,128)} %param.11) | data formatting | bytes 64 | tf_op args[3]
  3.2 0.8 %copy.13.offsets_ref = s32[8,8,2]{2,1,0:T(8,128)S(1)} copy(s32[8,8,2]{1,2,0:T(2,128)} %param.12) | data formatting | bytes 1024 | tf_op args[4]
  4.1 0.8 %copy.14.centre_ref = f32[8,2]{1,0:T(8,128)S(1)} copy(f32[8,2]{0,1:T(2,128)} %param.13) | data formatting | bytes 128 | tf_op args[5]
  4.8 0.1 pad.5.clone
  4.9 0.1 broadcast_in_dim.4
  5.0 0.8 %maximum_maximum_fusion.pack_ref = bf16[8,16,128]{2,1,0:T(8,128)(2,1)S(1)} fusion(bf16[8,1,128]{2,1,0:T(2,128)(2,1)S(1)} %broadcast_in_dim.4, bf16[8,2,128]{2,1,0:T(2,128)(2,1)} %param.9, bf16[8,8,128]{2,1,0:T(8,128)(2,1)S(1)} %bitcast.16, bf16[16]{0:T(256)(128)(2,1)S(1)} %pad.5.clone), kind=kLoop, calls=%fused_computation.2 | loop fusion | flops 131072 | bytes 55328 | tf_op jit(solution)/shard_map/concatenate | solution.py:278
  5.8 42.4 %route.1 = (bf16[8,11,16,128]{3,2,1,0:T(8,128)(2,1)S(1)}, bf16[8,2,4,128,128]{4,3,2,1,0:T(8,128)(2,1)S(1)}) custom-call(bf16[8,16,128]{2,1,0:T(8,128)(2,1)S(1)} %maximum_maximum_fusion.pack_ref, s32[8,1]{1,0:T(8,128)S(1)} %copy.12.group_ref, bf16[4,128,128]{2,1,0:T(8,128)(2,1)S(1)} %pad_maximum_fusion.tab_ref), custom_call_target="tpu_custom_call" | custom-call | tf_op jit(solution)/shard_map/route/pallas_call | solution.py:294
  48.1 13.3 %grid.1 = (f32[64,256]{1,0:T(8,128)S(1)}, f32[64,256]{1,0:T(8,128)S(1)}) custom-call(bf16[8,11,16,128]{3,2,1,0:T(8,128)(2,1)S(1)} %get-tuple-element.9.blocks_ref, s32[8,8,2]{2,1,0:T(8,128)S(1)} %copy.13.offsets_ref, f32[8,2]{1,0:T(8,128)S(1)} %copy.14.centre_ref, bf16[8,2,4,128,128]{4,3,2,1,0:T(8,128)(2,1)S(1)} %get-tuple-element.10.tabs_hbm), custom_call_target="tpu_custom_call" | custom-call | tf_op jit(solution)/shard_map/grid/pallas_call | solution.py:314
  61.4 2.7 %collective-permute-start = (f32[64,256]{1,0:T(8,128)S(1)}, f32[64,256]{1,0:T(8,128)S(1)}, u32[]{:S(2)}, u32[]{:S(2)}) collective-permute-start(f32[64,256]{1,0:T(8,128)S(1)} %get-tuple-element.12), channel_id=1, source_target_pairs={{0,1},{1,0},{2,3},{3,2},{4,5},{5,4},{6,7},{7,6},{8,9},{9,8},{10,11... | collective-permute-start | bytes 196616 | tf_op jit(solution)/shard_map/ppermute | solution.py:335
  64.1 0.0 copy-done
  64.1 0.1 dynamic-slice_bitcast_fusion
  64.1 0.1 multiply_multiply_fusion
  64.2 3.0 %collective-permute-done = f32[64,256]{1,0:T(8,128)S(1)} collective-permute-done((f32[64,256]{1,0:T(8,128)S(1)}, f32[64,256]{1,0:T(8,128)S(1)}, u32[]{:S(2)}, u32[]{:S(2)}) %collective-permute-start) | collective-permute-done | bytes 65568 | tf_op jit(solution)/shard_map/ppermute | solution.py:335
  67.3 0.7 broadcast_multiply_fusion
  (6 shorter events, 0.1 us)
Async XLA Ops:
  0.0 64.1 %copy-start = (f32[1,2,128]{2,1,0:T(2,128)S(1)}, f32[1,2,128]{2,1,0:T(2,128)}, u32[]{:S(2)}) copy-start(f32[1,2,128]{2,1,0:T(2,128)} %param.15) | copy-start | bytes 3076
  61.4 5.8 %collective-permute-start = (f32[64,256]{1,0:T(8,128)S(1)}, f32[64,256]{1,0:T(8,128)S(1)}, u32[]{:S(2)}, u32[]{:S(2)}) collective-permute-start(f32[64,256]{1,0:T(8,128)S(1)} %get-tuple-element.12), channel_id=1, source_target_pairs={{0,1},{1,0},{2,3},{3,2},{4,5},{5,4},{6,7},{7,6},{8,9},{9,8},{10,11... | collective-permute-start | bytes 196616 | tf_op jit(solution)/shard_map/ppermute | solution.py:335

commit v2 on v1

v2 whole, which is shorter than its diff:
```python
import math

import jax
import jax.numpy as jnp
from jax import lax
from jax.experimental import pallas as pl
from jax.experimental.pallas import tpu as pltpu
from jax.sharding import PartitionSpec as P

SU = 128
CH = 8
SPREAD = 1.5
ROOT = math.sqrt(math.log2(math.e) / (2.0 * SPREAD * SPREAD))
MESH = pl.DeviceIdType.MESH
F32 = jnp.float32
BF16 = jnp.bfloat16
TILES = 11
STEP = 4


def route_kernel(
    vis_ref, coord_ref, plane_hbm, group_hbm, raw_ref, blocks_ref, tabs_ref,
    plane_s, group_s, send, recv, stage, tab, a_send, a_recv, t_send, t_recv, v_send, v_recv, own_sem,
):
    f = lax.axis_index("facet")
    g = lax.axis_index("bl")
    c = lax.axis_index("chan")
    side = (f // 4) * 4
    y = lax.rem(f, 4)
    low = side + lax.rem(y + 3, 4)
    high = side + lax.rem(y + 1, 4)
    far = side + lax.rem(y + 2, 4)

    def flip(facet):
        return lax.rem(facet + 4, 8)

    up, down = (high, g, c), (low, g, c)
    beside, across = (flip(f), g, c), (flip(f), g, 1 - c)
    following = (f, lax.rem(g + 1, 8), c)

    barrier = pltpu.get_barrier_semaphore()
    for d in range(1, 8):
        for peer in ((f, lax.rem(g + d, 8), c), (lax.rem(f + d, 8), g, c)):
            pl.semaphore_signal(barrier, inc=1, device_id=peer, device_id_type=MESH)
    pl.semaphore_signal(barrier, inc=1, device_id=across, device_id_type=MESH)

    names = [
        pltpu.make_async_copy(plane_hbm, plane_s, own_sem.at[0]),
        pltpu.make_async_copy(group_hbm, group_s, own_sem.at[1]),
    ]
    for copy in names:
        copy.start()

    wide = (2 * SU, 2 * SU)
    to = lax.broadcasted_iota(jnp.int32, wide, 0)
    source = jnp.where(to < SU, 2 * to, 2 * to - (2 * SU - 1))
    pick = (source == lax.broadcasted_iota(jnp.int32, wide, 1)).astype(F32).astype(BF16)
    first = lax.dot_general(
        raw_ref[0], pick, (((0,), (1,)), ((), ())), preferred_element_type=F32
    ).astype(BF16)
    second = jnp.dot(pick, raw_ref[1], preferred_element_type=F32).astype(BF16)
    tab[0], tab[1] = first[:, :SU], first[:, SU:]
    tab[2], tab[3] = second[:SU], second[SU:]

    for copy in names:
        copy.wait()
    labels = [group_s[n, 0] for n in range(8)]
    rows = lax.broadcasted_iota(jnp.int32, (16, SU), 0)

    def build(group, carry):
        zero = jnp.int32(0)
        i0, i1, n0, n1 = zero, zero, zero, zero
        for n in reversed(range(8)):
            match = labels[n] == group
            i1 = jnp.where(match, i0, i1)
            n1 = jnp.where(match, n0, n1)
            i0 = jnp.where(match, n, i0)
            n0 = jnp.where(match, 1, n0)
        one = vis_ref[i0].astype(F32) * n0.astype(F32)
        two = vis_ref[i1].astype(F32) * n1.astype(F32)
        send[group, 0] = jnp.concatenate([one, two], axis=0).astype(BF16)
        misc = jnp.zeros((16, SU), F32)
        for k, at, here in ((0, i0, n0), (1, i1, n1)):
            spot = coord_ref[at].astype(F32)
            misc = jnp.where(rows == 3 * k, spot[0:1], misc)
            misc = jnp.where(rows == 3 * k + 1, spot[1:2], misc)
            misc = jnp.where(rows == 3 * k + 2, ((plane_s[at] + 1) * here).astype(F32), misc)
        send[group, 1] = misc.astype(BF16)
        return carry

    lax.fori_loop(0, 8, build, 0)
    pl.semaphore_wait(barrier, 15)

    def remote(sems, k, src, dst, peer):
        return pltpu.make_async_remote_copy(
            src_ref=src, dst_ref=dst, send_sem=sems[0].at[k], recv_sem=sems[1].at[k],
            device_id=peer, device_id_type=MESH,
        )

    started = []

    def go(sems, k, src, dst, peer):
        copy = remote(sems, k, src, dst, peer)
        copy.start()
        started.append(copy)

    def landed(sems, k, where):
        remote(sems, k, where, where, up).wait_recv()

    tables, visits = (t_send, t_recv), (v_send, v_recv)

    def column(facet, shift=0, half=None):
        whole = tabs_ref.at[facet, shift]
        return whole if half is None else whole.at[pl.ds(2 * half, 2)]

    def block(facet, half=None):
        whole = blocks_ref.at[facet]
        return whole if half is None else whole.at[pl.ds(6 * half, 6 - half)]

    def t_go(k, facet, peer, half=None):
        go(tables, k, column(facet, 0, half), column(facet, 0, half), peer)

    def t_shift(k, facet):
        go(tables, k, column(facet), column(facet, 1), following)

    def t_landed(k, facet, half=None):
        landed(tables, k, column(facet, 0, half))

    def v_go(k, facet, peer, half=None):
        go(visits, k, block(facet, half), block(facet, half), peer)

    def v_landed(k, facet, half=None):
        landed(visits, k, block(facet, half))

    for d in range(1, 8):
        peer = lax.rem(g + d, 8)
        copy = pltpu.make_async_remote_copy(
            src_ref=send.at[peer], dst_ref=recv.at[g], send_sem=a_send.at[d],
            recv_sem=a_recv.at[g], device_id=(f, peer, c), device_id_type=MESH,
        )
        copy.start()
        started.append(copy)
    go(tables, 0, tab, column(f), up)
    go(tables, 1, tab, column(f), down)
    go(tables, 2, tab.at[pl.ds(0, 2)], column(f, 0, 0), beside)
    go(tables, 3, tab.at[pl.ds(2, 2)], column(f, 0, 1), across)
    go(tables, 4, tab, column(f, 1), following)
    own_tab = pltpu.make_async_copy(tab, column(f), own_sem.at[0])
    own_tab.start()
    recv[g] = send[g]
    for d in range(1, 8):
        peer = lax.rem(g + d, 8)
        pltpu.make_async_remote_copy(
            src_ref=send.at[peer], dst_ref=recv.at[peer], send_sem=a_send.at[d],
            recv_sem=a_recv.at[peer], device_id=(f, peer, c), device_id_type=MESH,
        ).wait_recv()

    extra = [jnp.zeros((16, SU), F32) for _ in range(3)]
    for b in range(8):
        stage[b] = recv[b, 0]
        misc = recv[b, 1].astype(F32)
        for k in range(2):
            here = rows == 2 * b + k
            for e in range(3):
                line = 3 * k + e
                extra[e] = jnp.where(here, misc[line : line + 1], extra[e])
    for e in range(3):
        stage[8 + e] = extra[e].astype(BF16)
    go(visits, 0, stage, block(f), beside)
    go(visits, 1, stage, block(f), up)
    go(visits, 2, stage, block(f), down)
    own_blocks = pltpu.make_async_copy(stage, block(f), own_sem.at[1])
    own_blocks.start()

    t_landed(0, low)
    t_go(5, low, up, 0)
    t_go(6, low, beside, 0)
    t_go(7, low, across, 1)
    t_shift(8, low)
    t_landed(1, high)
    t_go(9, high, down, 1)
    t_go(10, high, beside, 0)
    t_go(11, high, across, 1)
    t_shift(12, high)
    v_landed(0, flip(f))
    v_go(5, flip(f), up)
    v_go(6, flip(f), down)
    v_landed(1, low)
    v_go(3, low, up, 0)
    v_landed(2, high)
    v_go(4, high, down, 1)
    t_landed(2, flip(f), 0)
    t_landed(3, flip(f), 1)
    t_shift(16, flip(f))
    v_landed(5, flip(low))
    v_go(7, flip(low), up, 0)
    v_landed(6, flip(high))
    v_go(8, flip(high), down, 1)
    t_landed(5, far, 0)
    t_go(13, far, beside, 0)
    t_landed(9, far, 1)
    t_go(14, far, across, 1)
    t_shift(15, far)
    t_landed(6, flip(low), 0)
    t_landed(7, flip(low), 1)
    t_shift(17, flip(low))
    t_landed(10, flip(high), 0)
    t_landed(11, flip(high), 1)
    t_shift(18, flip(high))
    t_landed(13, flip(far), 0)
    t_landed(14, flip(far), 1)
    t_shift(19, flip(far))
    v_landed(3, far, 0)
    v_landed(4, far, 1)
    v_landed(7, flip(far), 0)
    v_landed(8, flip(far), 1)
    for k, facet in ((4, f), (8, low), (12, high), (15, far)):
        landed(tables, k, column(facet, 1))
    for k, facet in ((16, f), (17, low), (18, high), (19, far)):
        landed(tables, k, column(flip(facet), 1))
    own_tab.wait()
    own_blocks.wait()
    for copy in started:
        copy.wait_send()


def sine_of_turns(turns):
    part = turns - jnp.floor(turns + 0.5)
    part = jnp.maximum(jnp.minimum(part, 0.5 - part), -0.5 - part)
    angle = part * (2.0 * math.pi)
    square = angle * angle
    total = jnp.full_like(angle, -1.0 / math.factorial(11))
    for power in (9, 7, 5, 3, 1):
        sign = 1.0 if power % 4 == 1 else -1.0
        total = total * square + sign / math.factorial(power)
    return total * angle


def grid_kernel(
    blocks_ref, offsets_hbm, centre_hbm, tabs_hbm, keep_ref, give_ref,
    offsets_ref, centre_ref, vis, line_u, line_v, order_v, order, turned, spots, planes, tabs, raw, sems,
):
    f = lax.axis_index("facet")
    g = lax.axis_index("bl")
    c = lax.axis_index("chan")
    fetch = pltpu.make_async_copy(tabs_hbm, tabs, sems.at[0])
    fetch.start()
    names = [
        pltpu.make_async_copy(offsets_hbm, offsets_ref, sems.at[2]),
        pltpu.make_async_copy(centre_hbm, centre_ref, sems.at[3]),
    ]
    for copy in names:
        copy.start()

    sub = lax.broadcasted_iota(jnp.int32, (SU, SU), 0)
    lane = lax.broadcasted_iota(jnp.int32, (SU, SU), 1)
    label = jnp.concatenate([blocks_ref[i, 10] for i in range(8)], axis=0)
    label = label.astype(F32).astype(jnp.int32) - 1
    number = (label >> 3) * 2 + jnp.where((label & 7) == g, 0, 1)
    number = jnp.where(label >= 0, number, 16).astype(F32)
    across = number.T
    ahead = (across < number) | ((across == number) & (lane < sub))
    place = jnp.sum(jnp.where(ahead, 1.0, 0.0), axis=1, keepdims=True)
    hit = place == lane.astype(F32)
    lines = [
        jnp.sum(jnp.where(hit, sub.astype(F32), 0.0), axis=0, keepdims=True),
        jnp.sum(jnp.where(hit, number, 0.0), axis=0, keepdims=True),
        jnp.sum(jnp.where(number < 16.0, 1.0, 0.0), axis=0, keepdims=True),
        jnp.zeros((5, SU), F32),
    ]
    order_v[...] = jnp.concatenate(lines, axis=0).astype(jnp.int32)
    orders = pltpu.make_async_copy(order_v, order, sems.at[1])
    orders.start()

    for i in range(8):
        line_u[16 * i : 16 * i + 16] = blocks_ref[i, 8].astype(F32)
        line_v[16 * i : 16 * i + 16] = blocks_ref[i, 9].astype(F32)
        for b in range(8):
            both = blocks_ref[i, b].astype(F32)
            vis[16 * i + 2 * b] = both[:8]
            vis[16 * i + 2 * b + 1] = both[8:]
    planes[...] = jnp.zeros_like(planes)
    orders.wait()
    for copy in names:
        copy.wait()
    steps = (order[2, 0] + STEP - 1) // STEP

    off_u = offsets_ref[f, g, 0].astype(F32)
    off_v = offsets_ref[f, g, 1].astype(F32)
    dir_l = centre_ref[f, 0]
    dir_m = centre_ref[f, 1]
    row = lax.broadcasted_iota(jnp.int32, (8, SU), 0)
    even = (row & 1) == 0
    channel = (c * 4 + (row >> 1)).astype(F32)
    scale = 1.0 + 0.01 * (channel - 0.5 * (CH - 1))

    def swap(pair):
        return jnp.where(even, pltpu.roll(pair, 7, 0), pltpu.roll(pair, 1, 0))

    def prepare(step, carry):
        for q in range(STEP):
            at = step * STEP + q
            slot = order[0, at]
            u = line_u[pl.ds(slot, 1), :]
            v = line_v[pl.ds(slot, 1), :]
            along = jnp.where(even, scale * u - off_u, scale * v - off_v)
            spots[at] = along * ROOT
            turns = (scale * (u * dir_l + v * dir_m)) * (1.0 / SU)
            turns = turns - jnp.floor(turns + 0.5)
            wave = sine_of_turns(turns + jnp.where(even, 0.25, 0.0))
            data = vis[slot]
            straight = data * wave
            crossed = data * swap(wave)
            turned[at] = jnp.where(even, straight - swap(straight), crossed + swap(crossed))
        return carry

    lax.fori_loop(0, steps, prepare, 0)

    cells = sub.astype(F32) * ROOT

    def profile(line):
        apart = line - cells
        return jnp.exp2(-(apart * apart)).astype(BF16)

    def gather(step, carry):
        for q in range(STEP):
            at = step * STEP + q
            along_u, real, imag = [], [], []
            for ch in range(4):
                along_u.append(profile(spots[at, 2 * ch : 2 * ch + 1, :]))
                along_v = profile(spots[at, 2 * ch + 1 : 2 * ch + 2, :])
                real.append(along_v * turned[at, 2 * ch : 2 * ch + 1, :].astype(BF16))
                imag.append(along_v * turned[at, 2 * ch + 1 : 2 * ch + 2, :].astype(BF16))
            left = jnp.concatenate(along_u, axis=1)
            right = jnp.concatenate(
                [jnp.concatenate(real, axis=1), jnp.concatenate(imag, axis=1)], axis=0
            )
            planes[order[1, at]] += lax.dot_general(
                left, right, (((1,), (1,)), ((), ())), preferred_element_type=F32
            )
        return carry

    lax.fori_loop(0, steps, gather, 0)
    fetch.wait()

    def turn(re, im):
        return jnp.concatenate(
            [jnp.concatenate([re, im], axis=1), jnp.concatenate([-im, re], axis=1)], axis=0
        )

    total = jnp.zeros((SU, 2 * SU), F32)
    for p in range(16):
        tab = tabs.at[p // 2, p % 2]
        part = jnp.dot(
            planes[p].astype(BF16), turn(tab[2], tab[3]), preferred_element_type=F32
        ).astype(BF16)
        total = total + jnp.dot(
            jnp.concatenate([tab[0], tab[1]], axis=1),
            turn(part[:, :SU], part[:, SU:]),
            preferred_element_type=F32,
        )
    raw[...] = total
    keep_ref[...] = raw[pl.ds(pl.multiple_of(c * 64, 64), 64), :]
    give_ref[...] = raw[pl.ds(pl.multiple_of((1 - c) * 64, 64), 64), :]


def body(
    visibilities, coords, plane_index, block_group, offsets, facet_centre, tables, antenna_gain
):
    held = visibilities.shape[0]
    norm = SU / math.sqrt(visibilities.shape[3] * held * 8 * CH)
    vmem = pl.BlockSpec(memory_space=pltpu.VMEM)
    hbm = pl.BlockSpec(memory_space=pl.ANY)
    dma = pltpu.SemaphoreType.DMA
    blocks, tabs = pl.pallas_call(
        route_kernel,
        out_shape=(
            jax.ShapeDtypeStruct((8, TILES, 16, SU), BF16),
            jax.ShapeDtypeStruct((8, 2, 4, SU, SU), BF16),
        ),
        in_specs=[vmem, vmem, hbm, hbm, vmem],
        out_specs=(hbm, hbm),
        scratch_shapes=[
            pltpu.SMEM((held,), jnp.int32),
            pltpu.SMEM((held, 1), jnp.int32),
            pltpu.VMEM((8, 2, 16, SU), BF16),
            pltpu.VMEM((8, 2, 16, SU), BF16),
            pltpu.VMEM((TILES, 16, SU), BF16),
            pltpu.VMEM((4, SU, SU), BF16),
            dma((8,)), dma((8,)), dma((20,)), dma((20,)), dma((9,)), dma((9,)), dma((2,)),
        ],
        compiler_params=pltpu.CompilerParams(
            collective_id=0, has_side_effects=True, vmem_limit_bytes=16 * 2**20
        ),
        name="route",
    )(
        visibilities.reshape(held, 8, SU), coords, plane_index, block_group,
        tables.reshape(2, 2 * SU, SU),
    )
    half = jax.ShapeDtypeStruct((64, 2 * SU), F32)
    keep, give = pl.pallas_call(
        grid_kernel,
        out_shape=(half, half),
        in_specs=[vmem, hbm, hbm, hbm],
        out_specs=(vmem, vmem),
        scratch_shapes=[
            pltpu.SMEM((8, 8, 2), jnp.int32),
            pltpu.SMEM((8, 2), F32),
            pltpu.VMEM((128, 8, SU), F32),
            pltpu.VMEM((128, SU), F32),
            pltpu.VMEM((128, SU), F32),
            pltpu.VMEM((8, SU), jnp.int32),
            pltpu.SMEM((8, SU), jnp.int32),
            pltpu.VMEM((128, 8, SU), F32),
            pltpu.VMEM((128, 8, SU), F32),
            pltpu.VMEM((17, SU, 2 * SU), F32),
            pltpu.VMEM((8, 2, 4, SU, SU), BF16),
            pltpu.VMEM((SU, 2 * SU), F32),
            dma((4,)),
        ],
        compiler_params=pltpu.CompilerParams(vmem_limit_bytes=32 * 2**20),
        name="grid",
    )(blocks, offsets, facet_centre, tabs)
    came = lax.ppermute(give, "chan", [(0, 1), (1, 0)])
    gain_u = lax.dynamic_slice_in_dim(antenna_gain[0, 0], lax.axis_index("chan") * 64, 64)
    gains = gain_u[:, None, None] * antenna_gain[0, 1][None, None, :] * norm
    result = (keep + came).reshape(64, 2, SU) * gains
    return result.reshape(1, 1, 64, 2, SU)


def solution(mesh):
    in_specs = (
        P(("facet", "bl"), "chan", None, None),
        P(("facet", "bl"), None, None),
        P(("facet", "bl")),
        P(("facet", "bl"), None),
        P(),
        P(),
        P(("facet", "bl"), None, None, None, None),
        P("bl", None, None),
    )
    out_specs = P("facet", "bl", "chan", None, None)
    return jax.shard_map(body, mesh=mesh, in_specs=in_specs, out_specs=out_specs, check_vma=False)
```

time: 68.7 us -> 49.4 us (0.72)
  Pallas kernels: 55.6 us -> 37.3 us
  other arithmetic: 2.19 us -> 0.75 us
  local copies, waits for them, and re-layouts: 4.4 us -> 5.38 us
    pallas_call x1, Pallas kernels: 42.4 us -> 24 us  [body(): pl.pallas_call(route_kernel, out_shape=(jax.ShapeDtypeStruct((8, TILES, 1...]
    unnamed x7 -> x13, local copies, waits for them, and re-layouts: 2.43 us -> 5.27 us
    slice x1 -> x0, local copies, waits for them, and re-layouts: 0.98 us -> none  [body(): tables[0, 0].transpose(1, 2, 0)]
    concatenate x2 -> x0, other arithmetic: 0.78 us -> none  [the longest x1 0.77 us: body(): jnp.concatenate([visibilities.transpose(0, 2, 1, 3).reshape(held, 8, SU),...]
    transpose x1 -> x0, local copies, waits for them, and re-layouts: 0.73 us -> none  [body(): visibilities.transpose(0, 2, 1, 3).reshape(held, 8, SU)]
where the time goes in v2:
time: 49.4 us; the launch traced here: 49.1 us
  Pallas kernels  37.3 us (76%)
  local copies, waits for them, and re-layouts  5.38 us (11%)
  waiting for transfers between devices  3.18 us (6%)
  starting transfers between devices  2.51 us (5%)
  other arithmetic  0.75 us (2%)
    pallas_call x1, Pallas kernels, body(): pl.pallas_call(route_kernel, out_shape=(jax.ShapeDtypeStruct((8, TILES, 1...  24 us
    pallas_call x1, Pallas kernels, body(): pl.pallas_call(grid_kernel, out_shape=(half, half), in_specs=[vmem, hbm,...  13.2 us
    unnamed x13, local copies, waits for them, and re-layouts  5.27 us
    ppermute x1, waiting for transfers between devices, body(): came = lax.ppermute(give, 'chan', [(0, 1), (1, 0)])  3.18 us
    ppermute x1, starting transfers between devices, body(): came = lax.ppermute(give, 'chan', [(0, 1), (1, 0)])  2.51 us
  transfers between devices with their start and end apart: 1, of which 1 were waited for; matrix products, arithmetic and copies ran while one was open for 0% of the time, Pallas kernels for 0%

profile of v2, /device:TPU:0, one launch (start us, length us, event | category | flops | bytes accessed | tf_op | source)
XLA Modules:
  0.0 49.1 jit_solution(10882233793925596114)
XLA Ops:
  0.0 0.0 copy-start.4
  0.0 0.7 %copy.9.group_hbm = s32[8,1]{1,0:T(8,128)S(1)} copy(s32[8,1]{0,1:T(1,128)} %param.11) | data formatting | bytes 64 | tf_op args[3]
  0.7 0.8 %copy.10.offsets_hbm = s32[8,8,2]{2,1,0:T(8,128)S(1)} copy(s32[8,8,2]{1,2,0:T(2,128)} %param.12) | data formatting | bytes 1024 | tf_op args[4]
  1.6 0.8 %copy.11.centre_hbm = f32[8,2]{1,0:T(8,128)S(1)} copy(f32[8,2]{0,1:T(2,128)} %param.13) | data formatting | bytes 128 | tf_op args[5]
  2.3 0.0 copy-start
  2.3 0.9 %copy-done = bf16[1,2,128,2,128]{4,3,2,1,0:T(2,128)(2,1)S(1)} copy-done((bf16[1,2,128,2,128]{4,3,2,1,0:T(2,128)(2,1)S(1)}, bf16[1,2,128,2,128]{4,3,2,1,0:T(2,128)(2,1)}, u32[]{:S(2)}) %copy-start) | copy-done | bytes 131096
  3.2 0.0 copy-start.1
  3.2 0.7 %copy-done.1 = bf16[8,4,2,128]{3,2,1,0:T(2,128)(2,1)S(1)} copy-done((bf16[8,4,2,128]{3,2,1,0:T(2,128)(2,1)S(1)}, bf16[8,4,2,128]{3,2,1,0:T(2,128)(2,1)}, u32[]{:S(2)}) %copy-start.1) | copy-done | bytes 16408
  3.9 0.0 copy-start.2
  3.9 0.7 %copy-done.2 = bf16[8,2,128]{2,1,0:T(2,128)(2,1)S(1)} copy-done((bf16[8,2,128]{2,1,0:T(2,128)(2,1)S(1)}, bf16[8,2,128]{2,1,0:T(2,128)(2,1)}, u32[]{:S(2)}) %copy-start.2) | copy-done | bytes 4120
  4.6 0.0 copy-start.3
  4.6 0.7 %copy-done.3 = s32[8]{0:T(128)S(1)} copy-done((s32[8]{0:T(128)S(1)}, s32[8]{0:T(128)}, u32[]{:S(2)}) %copy-start.3) | copy-done | bytes 56
  5.3 24.0 %route.1 = (bf16[8,11,16,128]{3,2,1,0:T(8,128)(2,1)S(1)}, bf16[8,2,4,128,128]{4,3,2,1,0:T(8,128)(2,1)S(1)}) custom-call(bf16[8,8,128]{2,1,0:T(8,128)(2,1)S(1)} %bitcast.7, bf16[8,2,128]{2,1,0:T(2,128)(2,1)S(1)} %copy-done.2, s32[8]{0:T(128)S(1)} %copy-done.3, s32[8,1]{1,0:T(8,128)S(1)} %copy.9.group_hbm, bf16[2,256,128]{2,1,0:T(8,128)(2,1)S(1)} %bitcast.6), custom_call_target="tpu_custom_call" | custom-call | tf_op jit(solution)/shard_map/route/pallas_call | solution.py:375
  29.3 13.2 %grid.1 = (f32[64,256]{1,0:T(8,128)S(1)}, f32[64,256]{1,0:T(8,128)S(1)}) custom-call(bf16[8,11,16,128]{3,2,1,0:T(8,128)(2,1)S(1)} %get-tuple-element.9.blocks_ref, s32[8,8,2]{2,1,0:T(8,128)S(1)} %copy.10.offsets_hbm, f32[8,2]{1,0:T(8,128)S(1)} %copy.11.centre_hbm, bf16[8,2,4,128,128]{4,3,2,1,0:T(8,128)(2,1)S(1)} %get-tuple-element.10.tabs_hbm), custom_call_target="tpu_custom_call" | custom-call | tf_op jit(solution)/shard_map/grid/pallas_call | solution.py:401
  42.6 2.5 %collective-permute-start = (f32[64,256]{1,0:T(8,128)S(1)}, f32[64,256]{1,0:T(8,128)S(1)}, u32[]{:S(2)}, u32[]{:S(2)}) collective-permute-start(f32[64,256]{1,0:T(8,128)S(1)} %get-tuple-element.12), channel_id=1, source_target_pairs={{0,1},{1,0},{2,3},{3,2},{4,5},{5,4},{6,7},{7,6},{8,9},{9,8},{10,11... | collective-permute-start | bytes 196616 | tf_op jit(solution)/shard_map/ppermute | solution.py:424
  45.1 0.0 copy-done.4
  45.1 0.1 dynamic-slice_bitcast_fusion
  45.2 0.1 multiply_multiply_fusion
  45.2 3.2 %collective-permute-done = f32[64,256]{1,0:T(8,128)S(1)} collective-permute-done((f32[64,256]{1,0:T(8,128)S(1)}, f32[64,256]{1,0:T(8,128)S(1)}, u32[]{:S(2)}, u32[]{:S(2)}) %collective-permute-start) | collective-permute-done | bytes 65568 | tf_op jit(solution)/shard_map/ppermute | solution.py:424
  48.5 0.7 %broadcast_multiply_fusion = f32[1,1,64,2,128]{4,3,2,1,0:T(2,128)} fusion(f32[1,1,64,2,128]{4,3,2,1,0:T(2,128)S(1)} %reshape.59, f32[64,128]{1,0:T(8,128)S(1)} %multiply_multiply_fusion), kind=kLoop, calls=%fused_computation | loop fusion | flops 16384 | bytes 163840 | tf_op jit(solution)/shard_map/mul | solution.py:427
  (3 shorter events, 0.0 us)
Async XLA Ops:
  0.0 45.1 %copy-start.4 = (f32[1,2,128]{2,1,0:T(2,128)S(1)}, f32[1,2,128]{2,1,0:T(2,128)}, u32[]{:S(2)}) copy-start(f32[1,2,128]{2,1,0:T(2,128)} %param.15) | copy-start | bytes 3076
  2.3 0.9 %copy-start = (bf16[1,2,128,2,128]{4,3,2,1,0:T(2,128)(2,1)S(1)}, bf16[1,2,128,2,128]{4,3,2,1,0:T(2,128)(2,1)}, u32[]{:S(2)}) copy-start(bf16[1,2,128,2,128]{4,3,2,1,0:T(2,128)(2,1)} %param.14) | copy-start | bytes 393220
  3.2 0.7 %copy-start.1 = (bf16[8,4,2,128]{3,2,1,0:T(2,128)(2,1)S(1)}, bf16[8,4,2,128]{3,2,1,0:T(2,128)(2,1)}, u32[]{:S(2)}) copy-start(bf16[8,4,2,128]{3,2,1,0:T(2,128)(2,1)} %param.8) | copy-start | bytes 49156
  3.9 0.7 %copy-start.2 = (bf16[8,2,128]{2,1,0:T(2,128)(2,1)S(1)}, bf16[8,2,128]{2,1,0:T(2,128)(2,1)}, u32[]{:S(2)}) copy-start(bf16[8,2,128]{2,1,0:T(2,128)(2,1)} %coord_ref.1) | copy-start | bytes 12292
  4.6 0.7 %copy-start.3 = (s32[8]{0:T(128)S(1)}, s32[8]{0:T(128)}, u32[]{:S(2)}) copy-start(s32[8]{0:T(128)} %plane_hbm.1) | copy-start | bytes 100
  42.6 5.8 %collective-permute-start = (f32[64,256]{1,0:T(8,128)S(1)}, f32[64,256]{1,0:T(8,128)S(1)}, u32[]{:S(2)}, u32[]{:S(2)}) collective-permute-start(f32[64,256]{1,0:T(8,128)S(1)} %get-tuple-element.12), channel_id=1, source_target_pairs={{0,1},{1,0},{2,3},{3,2},{4,5},{5,4},{6,7},{7,6},{8,9},{9,8},{10,11... | collective-permute-start | bytes 196616 | tf_op jit(solution)/shard_map/ppermute | solution.py:424

commit v3 on v2

--- a/solution.py
+++ b/solution.py
@@ -9,18 +9,19 @@
 
 SU = 128
 CH = 8
+NORM = SU / math.sqrt(128 * 8 * 8 * CH)
 SPREAD = 1.5
 ROOT = math.sqrt(math.log2(math.e) / (2.0 * SPREAD * SPREAD))
 MESH = pl.DeviceIdType.MESH
 F32 = jnp.float32
 BF16 = jnp.bfloat16
 TILES = 11
-STEP = 4
+STEP = 8
 
 
 def route_kernel(
-    vis_ref, coord_ref, plane_hbm, group_hbm, raw_ref, blocks_ref, tabs_ref,
-    plane_s, group_s, send, recv, stage, tab, a_send, a_recv, t_send, t_recv, v_send, v_recv, own_sem,
+    vis_hbm, coord_hbm, plane_hbm, group_hbm, raw_hbm, blocks_ref, tabs_ref,
+    vis_ref, coord_ref, plane_s, group_s, raw_ref, send, recv, stage, tab, a_send, a_recv, t_send, t_recv, v_send, v_recv, own_sem,
 ):
     f = lax.axis_index("facet")
     g = lax.axis_index("bl")
@@ -36,7 +37,6 @@
 
     up, down = (high, g, c), (low, g, c)
     beside, across = (flip(f), g, c), (flip(f), g, 1 - c)
-    following = (f, lax.rem(g + 1, 8), c)
 
     barrier = pltpu.get_barrier_semaphore()
     for d in range(1, 8):
@@ -44,9 +44,13 @@
             pl.semaphore_signal(barrier, inc=1, device_id=peer, device_id_type=MESH)
     pl.semaphore_signal(barrier, inc=1, device_id=across, device_id_type=MESH)
 
+    fetch_raw = pltpu.make_async_copy(raw_hbm, raw_ref, own_sem.at[2])
+    fetch_raw.start()
     names = [
+        pltpu.make_async_copy(group_hbm, group_s, own_sem.at[1]),
         pltpu.make_async_copy(plane_hbm, plane_s, own_sem.at[0]),
-        pltpu.make_async_copy(group_hbm, group_s, own_sem.at[1]),
+        pltpu.make_async_copy(vis_hbm, vis_ref, own_sem.at[3]),
+        pltpu.make_async_copy(coord_hbm, coord_ref, own_sem.at[4]),
     ]
     for copy in names:
         copy.start()
@@ -55,6 +59,7 @@
     to = lax.broadcasted_iota(jnp.int32, wide, 0)
     source = jnp.where(to < SU, 2 * to, 2 * to - (2 * SU - 1))
     pick = (source == lax.broadcasted_iota(jnp.int32, wide, 1)).astype(F32).astype(BF16)
+    fetch_raw.wait()
     first = lax.dot_general(
         raw_ref[0], pick, (((0,), (1,)), ((), ())), preferred_element_type=F32
     ).astype(BF16)
@@ -64,7 +69,7 @@
 
     for copy in names:
         copy.wait()
-    labels = [group_s[n, 0] for n in range(8)]
+    labels = [group_s[n] for n in range(8)]
     rows = lax.broadcasted_iota(jnp.int32, (16, SU), 0)
 
     def build(group, carry):
@@ -109,8 +114,8 @@
 
     tables, visits = (t_send, t_recv), (v_send, v_recv)
 
-    def column(facet, shift=0, half=None):
-        whole = tabs_ref.at[facet, shift]
+    def column(facet, half=None):
+        whole = tabs_ref.at[facet]
         return whole if half is None else whole.at[pl.ds(2 * half, 2)]
 
     def block(facet, half=None):
@@ -118,13 +123,10 @@
         return whole if half is None else whole.at[pl.ds(6 * half, 6 - half)]
 
     def t_go(k, facet, peer, half=None):
-        go(tables, k, column(facet, 0, half), column(facet, 0, half), peer)
-
-    def t_shift(k, facet):
-        go(tables, k, column(facet), column(facet, 1), following)
+        go(tables, k, column(facet, half), column(facet, half), peer)
 
     def t_landed(k, facet, half=None):
-        landed(tables, k, column(facet, 0, half))
+        landed(tables, k, column(facet, half))
 
     def v_go(k, facet, peer, half=None):
         go(visits, k, block(facet, half), block(facet, half), peer)
@@ -142,9 +144,8 @@
         started.append(copy)
     go(tables, 0, tab, column(f), up)
     go(tables, 1, tab, column(f), down)
-    go(tables, 2, tab.at[pl.ds(0, 2)], column(f, 0, 0), beside)
-    go(tables, 3, tab.at[pl.ds(2, 2)], column(f, 0, 1), across)
-    go(tables, 4, tab, column(f, 1), following)
+    go(tables, 2, tab.at[pl.ds(0, 2)], column(f, 0), beside)
+    go(tables, 3, tab.at[pl.ds(2, 2)], column(f, 1), across)
     own_tab = pltpu.make_async_copy(tab, column(f), own_sem.at[0])
     own_tab.start()
     recv[g] = send[g]
@@ -173,15 +174,13 @@
     own_blocks.start()
 
     t_landed(0, low)
-    t_go(5, low, up, 0)
-    t_go(6, low, beside, 0)
-    t_go(7, low, across, 1)
-    t_shift(8, low)
+    t_go(4, low, up, 0)
+    t_go(5, low, beside, 0)
+    t_go(6, low, across, 1)
     t_landed(1, high)
-    t_go(9, high, down, 1)
-    t_go(10, high, beside, 0)
-    t_go(11, high, across, 1)
-    t_shift(12, high)
+    t_go(7, high, down, 1)
+    t_go(8, high, beside, 0)
+    t_go(9, high, across, 1)
     v_landed(0, flip(f))
     v_go(5, flip(f), up)
     v_go(6, flip(f), down)
@@ -191,33 +190,24 @@
     v_go(4, high, down, 1)
     t_landed(2, flip(f), 0)
     t_landed(3, flip(f), 1)
-    t_shift(16, flip(f))
     v_landed(5, flip(low))
     v_go(7, flip(low), up, 0)
     v_landed(6, flip(high))
     v_go(8, flip(high), down, 1)
-    t_landed(5, far, 0)
-    t_go(13, far, beside, 0)
-    t_landed(9, far, 1)
-    t_go(14, far, across, 1)
-    t_shift(15, far)
-    t_landed(6, flip(low), 0)
-    t_landed(7, flip(low), 1)
-    t_shift(17, flip(low))
-    t_landed(10, flip(high), 0)
-    t_landed(11, flip(high), 1)
-    t_shift(18, flip(high))
-    t_landed(13, flip(far), 0)
-    t_landed(14, flip(far), 1)
-    t_shift(19, flip(far))
+    t_landed(4, far, 0)
+    t_go(10, far, beside, 0)
+    t_landed(7, far, 1)
+    t_go(11, far, across, 1)
+    t_landed(5, flip(low), 0)
+    t_landed(6, flip(low), 1)
+    t_landed(8, flip(high), 0)
+    t_landed(9, flip(high), 1)
+    t_landed(10, flip(far), 0)
+    t_landed(11, flip(far), 1)
     v_landed(3, far, 0)
     v_landed(4, far, 1)
     v_landed(7, flip(far), 0)
     v_landed(8, flip(far), 1)
-    for k, facet in ((4, f), (8, low), (12, high), (15, far)):
-        landed(tables, k, column(facet, 1))
-    for k, facet in ((16, f), (17, low), (18, high), (19, far)):
-        landed(tables, k, column(flip(facet), 1))
     own_tab.wait()
     own_blocks.wait()
     for copy in started:
@@ -237,17 +227,15 @@
 
 
 def grid_kernel(
-    blocks_ref, offsets_hbm, centre_hbm, tabs_hbm, keep_ref, give_ref,
-    offsets_ref, centre_ref, vis, line_u, line_v, order_v, order, turned, spots, planes, tabs, raw, sems,
+    blocks_ref, offsets_hbm, centre_hbm, sums_ref,
+    offsets_ref, centre_ref, vis, line_u, line_v, order_v, order, turned, spots, planes, sems,
 ):
     f = lax.axis_index("facet")
     g = lax.axis_index("bl")
     c = lax.axis_index("chan")
-    fetch = pltpu.make_async_copy(tabs_hbm, tabs, sems.at[0])
-    fetch.start()
     names = [
-        pltpu.make_async_copy(offsets_hbm, offsets_ref, sems.at[2]),
-        pltpu.make_async_copy(centre_hbm, centre_ref, sems.at[3]),
+        pltpu.make_async_copy(offsets_hbm, offsets_ref, sems.at[0]),
+        pltpu.make_async_copy(centre_hbm, centre_ref, sems.at[2]),
     ]
     for copy in names:
         copy.start()
@@ -285,10 +273,10 @@
         copy.wait()
     steps = (order[2, 0] + STEP - 1) // STEP
 
-    off_u = offsets_ref[f, g, 0].astype(F32)
-    off_v = offsets_ref[f, g, 1].astype(F32)
-    dir_l = centre_ref[f, 0]
-    dir_m = centre_ref[f, 1]
+    off_u = offsets_ref[f, 0, g].astype(F32)
+    off_v = offsets_ref[f, 1, g].astype(F32)
+    dir_l = centre_ref[0, f]
+    dir_m = centre_ref[1, f]
     row = lax.broadcasted_iota(jnp.int32, (8, SU), 0)
     even = (row & 1) == 0
     channel = (c * 4 + (row >> 1)).astype(F32)
@@ -329,8 +317,9 @@
             for ch in range(4):
                 along_u.append(profile(spots[at, 2 * ch : 2 * ch + 1, :]))
                 along_v = profile(spots[at, 2 * ch + 1 : 2 * ch + 2, :])
-                real.append(along_v * turned[at, 2 * ch : 2 * ch + 1, :].astype(BF16))
-                imag.append(along_v * turned[at, 2 * ch + 1 : 2 * ch + 2, :].astype(BF16))
+                for line, parts in ((2 * ch, real), (2 * ch + 1, imag)):
+                    weight = jnp.broadcast_to(turned[at, line : line + 1, :], (16, SU)).astype(BF16)
+                    parts.append((along_v.reshape(8, 16, SU) * weight[None]).reshape(SU, SU))
             left = jnp.concatenate(along_u, axis=1)
             right = jnp.concatenate(
                 [jnp.concatenate(real, axis=1), jnp.concatenate(imag, axis=1)], axis=0
@@ -341,71 +330,109 @@
         return carry
 
     lax.fori_loop(0, steps, gather, 0)
-    fetch.wait()
+    for p in range(16):
+        sums_ref[p] = planes[p].astype(BF16)
+
+
+def finish_kernel(
+    sums_ref, own_hbm, shifted, gain_hbm, out_ref, gain, own, parts, give, came, sems
+):
+    f = lax.axis_index("facet")
+    g = lax.axis_index("bl")
+    c = lax.axis_index("chan")
+    partner = (f, g, 1 - c)
+    barrier = pltpu.get_barrier_semaphore()
+    pl.semaphore_signal(barrier, inc=1, device_id=partner, device_id_type=MESH)
+    fetch = pltpu.make_async_copy(own_hbm, own, sems.at[0])
+    fetch.start()
+    gains = pltpu.make_async_copy(gain_hbm, gain, sems.at[3])
+    gains.start()
 
     def turn(re, im):
         return jnp.concatenate(
             [jnp.concatenate([re, im], axis=1), jnp.concatenate([-im, re], axis=1)], axis=0
         )
 
-    total = jnp.zeros((SU, 2 * SU), F32)
-    for p in range(16):
-        tab = tabs.at[p // 2, p % 2]
-        part = jnp.dot(
-            planes[p].astype(BF16), turn(tab[2], tab[3]), preferred_element_type=F32
-        ).astype(BF16)
-        total = total + jnp.dot(
-            jnp.concatenate([tab[0], tab[1]], axis=1),
-            turn(part[:, :SU], part[:, SU:]),
-            preferred_element_type=F32,
-        )
-    raw[...] = total
-    keep_ref[...] = raw[pl.ds(pl.multiple_of(c * 64, 64), 64), :]
-    give_ref[...] = raw[pl.ds(pl.multiple_of((1 - c) * 64, 64), 64), :]
+    for h, held in ((1, shifted), (0, own)):
+        if h == 0:
+            fetch.wait()
+        for i in range(8):
+            part = jnp.dot(
+                sums_ref[2 * i + h], turn(held[i, 2], held[i, 3]), preferred_element_type=F32
+            ).astype(BF16)
+            parts[8 * h + i] = turn(part[:, :SU], part[:, SU:])
+
+    def rows_of(half):
+        rows = pl.ds(pl.multiple_of(half * 64, 64), 64)
+        total = jnp.zeros((64, 2 * SU), F32)
+        for h, held in enumerate((own, shifted)):
+            for i in range(8):
+                matrix = jnp.concatenate([held[i, 0, rows], held[i, 1, rows]], axis=1)
+                total = total + jnp.dot(matrix, parts[8 * h + i], preferred_element_type=F32)
+        return total
+
+    give[...] = rows_of(1 - c)
+    pl.semaphore_wait(barrier, 1)
+    copy = pltpu.make_async_remote_copy(
+        src_ref=give, dst_ref=came, send_sem=sems.at[1], recv_sem=sems.at[2],
+        device_id=partner, device_id_type=MESH,
+    )
+    copy.start()
+    keep = rows_of(c)
+    gains.wait()
+    tall = (64, SU)
+    mine = lax.broadcasted_iota(jnp.int32, tall, 1) == lax.broadcasted_iota(jnp.int32, tall, 0) + c * 64
+    along_u = jnp.sum(jnp.where(mine, gain[0, 0:1], 0.0), axis=1, keepdims=True)
+    both = along_u * gain[0, 1:2] * NORM
+    copy.wait()
+    out_ref[...] = (keep + came[...]) * jnp.concatenate([both, both], axis=1)
 
 
 def body(
     visibilities, coords, plane_index, block_group, offsets, facet_centre, tables, antenna_gain
 ):
     held = visibilities.shape[0]
-    norm = SU / math.sqrt(visibilities.shape[3] * held * 8 * CH)
     vmem = pl.BlockSpec(memory_space=pltpu.VMEM)
-    hbm = pl.BlockSpec(memory_space=pl.ANY)
+    hbm = pl.BlockSpec(memory_space=pltpu.HBM)
+    loose = pl.BlockSpec(memory_space=pl.ANY)
     dma = pltpu.SemaphoreType.DMA
     blocks, tabs = pl.pallas_call(
         route_kernel,
         out_shape=(
             jax.ShapeDtypeStruct((8, TILES, 16, SU), BF16),
-            jax.ShapeDtypeStruct((8, 2, 4, SU, SU), BF16),
+            jax.ShapeDtypeStruct((8, 4, SU, SU), BF16),
         ),
-        in_specs=[vmem, vmem, hbm, hbm, vmem],
-        out_specs=(hbm, hbm),
+        in_specs=[hbm] * 5,
+        out_specs=(loose, loose),
         scratch_shapes=[
+            pltpu.VMEM((held, 8, SU), BF16),
+            pltpu.VMEM((held, 2, SU), BF16),
             pltpu.SMEM((held,), jnp.int32),
-            pltpu.SMEM((held, 1), jnp.int32),
+            pltpu.SMEM((held,), jnp.int32),
+            pltpu.VMEM((2, 2 * SU, SU), BF16),
             pltpu.VMEM((8, 2, 16, SU), BF16),
             pltpu.VMEM((8, 2, 16, SU), BF16),
             pltpu.VMEM((TILES, 16, SU), BF16),
             pltpu.VMEM((4, SU, SU), BF16),
-            dma((8,)), dma((8,)), dma((20,)), dma((20,)), dma((9,)), dma((9,)), dma((2,)),
+            dma((8,)), dma((8,)), dma((12,)), dma((12,)), dma((9,)), dma((9,)), dma((5,)),
         ],
         compiler_params=pltpu.CompilerParams(
-            collective_id=0, has_side_effects=True, vmem_limit_bytes=16 * 2**20
+            collective_id=0, has_side_effects=True, vmem_limit_bytes=60 * 2**20
         ),
         name="route",
     )(
-        visibilities.reshape(held, 8, SU), coords, plane_index, block_group,
+        visibilities.reshape(held, 8, SU), coords, plane_index, block_group.reshape(held),
         tables.reshape(2, 2 * SU, SU),
     )
-    half = jax.ShapeDtypeStruct((64, 2 * SU), F32)
-    keep, give = pl.pallas_call(
+    shifted = lax.ppermute(tabs, "bl", [(i, (i + 1) % 8) for i in range(8)])
+    sums = pl.pallas_call(
         grid_kernel,
-        out_shape=(half, half),
-        in_specs=[vmem, hbm, hbm, hbm],
-        out_specs=(vmem, vmem),
+        out_shape=jax.ShapeDtypeStruct((16, SU, 2 * SU), BF16),
+        in_specs=[vmem, hbm, hbm],
+        out_specs=vmem,
         scratch_shapes=[
-            pltpu.SMEM((8, 8, 2), jnp.int32),
-            pltpu.SMEM((8, 2), F32),
+            pltpu.SMEM((8, 2, 8), jnp.int32),
+            pltpu.SMEM((2, 8), F32),
             pltpu.VMEM((128, 8, SU), F32),
             pltpu.VMEM((128, SU), F32),
             pltpu.VMEM((128, SU), F32),
@@ -414,18 +441,33 @@
             pltpu.VMEM((128, 8, SU), F32),
             pltpu.VMEM((128, 8, SU), F32),
             pltpu.VMEM((17, SU, 2 * SU), F32),
-            pltpu.VMEM((8, 2, 4, SU, SU), BF16),
-            pltpu.VMEM((SU, 2 * SU), F32),
+            dma((3,)),
+        ],
+        compiler_params=pltpu.CompilerParams(vmem_limit_bytes=40 * 2**20),
+        cost_estimate=pl.CostEstimate(
+            flops=5 * 10**9, bytes_accessed=2 * 10**6, transcendentals=10**7
+        ),
+        name="grid",
+    )(blocks, offsets.transpose(0, 2, 1), facet_centre.T)
+    rows_sum = pl.pallas_call(
+        finish_kernel,
+        out_shape=jax.ShapeDtypeStruct((64, 2 * SU), F32),
+        in_specs=[vmem, hbm, vmem, hbm],
+        out_specs=vmem,
+        scratch_shapes=[
+            pltpu.VMEM((1, 2, SU), F32),
+            pltpu.VMEM((8, 4, SU, SU), BF16),
+            pltpu.VMEM((16, 2 * SU, 2 * SU), BF16),
+            pltpu.VMEM((64, 2 * SU), F32),
+            pltpu.VMEM((64, 2 * SU), F32),
             dma((4,)),
         ],
-        compiler_params=pltpu.CompilerParams(vmem_limit_bytes=32 * 2**20),
-        name="grid",
-    )(blocks, offsets, facet_centre, tabs)
-    came = lax.ppermute(give, "chan", [(0, 1), (1, 0)])
-    gain_u = lax.dynamic_slice_in_dim(antenna_gain[0, 0], lax.axis_index("chan") * 64, 64)
-    gains = gain_u[:, None, None] * antenna_gain[0, 1][None, None, :] * norm
-    result = (keep + came).reshape(64, 2, SU) * gains
-    return result.reshape(1, 1, 64, 2, SU)
+        compiler_params=pltpu.CompilerParams(
+            collective_id=1, has_side_effects=True, vmem_limit_bytes=24 * 2**20
+        ),
+        name="finish",
+    )(sums, tabs, shifted, antenna_gain)
+    return rows_sum.reshape(1, 1, 64, 2, SU)
 
 
 def solution(mesh):

time: 49.4 us -> 45 us (0.911)
  local copies, waits for them, and re-layouts: 5.38 us -> 2.32 us
  starting transfers between devices: 2.51 us -> 0.02 us
  Pallas kernels: 37.3 us -> 39.6 us
  other arithmetic: 0.75 us -> 0 us
    pallas_call x1 -> x2, Pallas kernels: 13.2 us -> 17 us  [the longest x1 11.2 us: body(): pl.pallas_call(grid_kernel, out_shape=jax.ShapeDtypeStruct((16, SU, 2 * S...]
    unnamed x13 -> x10, local copies, waits for them, and re-layouts: 5.27 us -> 1.66 us
    ppermute x1, starting transfers between devices: 2.51 us -> 0.02 us  [body(): shifted = lax.ppermute(tabs, 'bl', [(i, (i + 1) % 8) for i in range(8)])]
    pallas_call x1, Pallas kernels: 24 us -> 22.6 us  [body(): pl.pallas_call(route_kernel, out_shape=(jax.ShapeDtypeStruct((8, TILES, 1...]
    mul x2 -> x0, other arithmetic: 0.74 us -> none  [the longest x1 0.67 us: body(): result = (keep + came).reshape(64, 2, SU) * gains]
    reshape x1, local copies, waits for them, and re-layouts: 0.04 us -> 0.66 us  [body(): return rows_sum.reshape(1, 1, 64, 2, SU)]
  transfers between devices with their start and end apart: 1 -> 1, of which waited for: 1 -> 1; matrix products, arithmetic and copies ran while one was open for 0% -> 0% of each run, Pallas kernels for 0% -> 25%
where the time goes in v3:
time: 45 us; the launch traced here: 44.8 us
  Pallas kernels  39.6 us (88%)
  waiting for transfers between devices  2.8 us (6%)
  local copies, waits for them, and re-layouts  2.32 us (5%)
    pallas_call x1, Pallas kernels, body(): pl.pallas_call(route_kernel, out_shape=(jax.ShapeDtypeStruct((8, TILES, 1...  22.6 us
    pallas_call x1, Pallas kernels, body(): pl.pallas_call(grid_kernel, out_shape=jax.ShapeDtypeStruct((16, SU, 2 * S...  11.2 us
    pallas_call x1, Pallas kernels, body(): pl.pallas_call(finish_kernel, out_shape=jax.ShapeDtypeStruct((64, 2 * SU)...  5.82 us
    ppermute x1, waiting for transfers between devices, body(): shifted = lax.ppermute(tabs, 'bl', [(i, (i + 1) % 8) for i in range(8)])  2.8 us
    unnamed x10, local copies, waits for them, and re-layouts  1.66 us
  transfers between devices with their start and end apart: 1, of which 1 were waited for; matrix products, arithmetic and copies ran while one was open for 0% of the time, Pallas kernels for 25%

profile of v3, /device:TPU:0, one launch (start us, length us, event | category | flops | bytes accessed | tf_op | source)
XLA Modules:
  0.0 44.8 jit_solution(7212973796366552930)
XLA Ops:
  0.0 0.0 copy-start.3
  0.0 22.6 %route.1 = (bf16[8,11,16,128]{3,2,1,0:T(8,128)(2,1)}, bf16[8,4,128,128]{3,2,1,0:T(8,128)(2,1)}) custom-call(bf16[8,8,128]{2,1,0:T(8,128)(2,1)} %bitcast.8, bf16[8,2,128]{2,1,0:T(2,128)(2,1)} %coord_hbm.1, s32[8]{0:T(128)} %plane_hbm.1, s32[8]{0:T(128)} %bitcast.9, bf16[2,256,128]{2,1,0:T(8,128)(2,1)} %bitcast.7), custom_call_target="tpu_custom_call" | custom-call | tf_op jit(solution)/shard_map/route/pallas_call | solution.py:399
  22.6 0.0 collective-permute-start
  22.7 0.0 copy-start.4
  22.7 0.0 copy-done.3
  22.7 0.7 %copy-done.4 = f32[8,2]{0,1:T(2,128)S(1)} copy-done((f32[8,2]{0,1:T(2,128)S(1)}, f32[8,2]{0,1:T(2,128)}, u32[]{:S(2)}) %copy-start.4) | copy-done | bytes 88
  23.3 0.0 copy-start.2
  23.3 1.0 %copy-done.2 = bf16[8,11,16,128]{3,2,1,0:T(8,128)(2,1)S(1)} copy-done((bf16[8,11,16,128]{3,2,1,0:T(8,128)(2,1)S(1)}, bf16[8,11,16,128]{3,2,1,0:T(8,128)(2,1)}, u32[]{:S(2)}) %copy-start.2) | copy-done | bytes 360472
  24.3 0.0 copy-start
  24.3 0.0 copy-start.1
  24.3 11.2 %grid.1.sums_ref = bf16[16,128,256]{2,1,0:T(8,128)(2,1)S(1)} custom-call(bf16[8,11,16,128]{3,2,1,0:T(8,128)(2,1)S(1)} %copy-done.2, s32[8,2,8]{2,1,0:T(2,128)S(1)} %bitcast.5, f32[2,8]{1,0:T(2,128)S(1)} %bitcast.6), custom_call_target="tpu_custom_call" | custom-call | flops 5000000000 | bytes 2000000 | tf_op jit(solution)/shard_map/grid/pallas_call | solution.py:428
  35.5 2.8 %collective-permute-done.shifted = bf16[8,4,128,128]{3,2,1,0:T(8,128)(2,1)S(1)} collective-permute-done((bf16[8,4,128,128]{3,2,1,0:T(8,128)(2,1)}, bf16[8,4,128,128]{3,2,1,0:T(8,128)(2,1)S(1)}, u32[]{:S(2)}, u32[]{:S(2)}) %collective-permute-start) | collective-permute-done | bytes 1048608 | tf_op jit(solution)/shard_map/ppermute | solution.py:427
  38.3 0.0 copy-done
  38.3 0.0 copy-done.1
  38.3 5.8 %finish.1 = f32[64,256]{1,0:T(8,128)S(1)} custom-call(bf16[16,128,256]{2,1,0:T(8,128)(2,1)S(1)} %grid.1.sums_ref, bf16[8,4,128,128]{3,2,1,0:T(8,128)(2,1)S(1)} %copy-done, bf16[8,4,128,128]{3,2,1,0:T(8,128)(2,1)S(1)} %collective-permute-done.shifted, f32[1,2,128]{2,1,0:T(2,128)S(1)} %copy-done.1), custom_call_target="tpu_custom_call" | custom-call | tf_op jit(solution)/shard_map/finish/pallas_call | solution.py:452
  44.1 0.7 %reshape.15 = f32[1,1,64,2,128]{4,3,2,1,0:T(2,128)} reshape(f32[64,256]{1,0:T(8,128)S(1)} %finish.1) | data formatting | bytes 131072 | tf_op jit(solution)/shard_map/reshape | solution.py:470
Async XLA Ops:
  0.0 22.7 %copy-start.3 = (s32[8,8,2]{1,2,0:T(2,128)S(1)}, s32[8,8,2]{1,2,0:T(2,128)}, u32[]{:S(2)}) copy-start(s32[8,8,2]{1,2,0:T(2,128)} %param.12) | copy-start | bytes 1540
  22.6 15.7 %collective-permute-start = (bf16[8,4,128,128]{3,2,1,0:T(8,128)(2,1)}, bf16[8,4,128,128]{3,2,1,0:T(8,128)(2,1)S(1)}, u32[]{:S(2)}, u32[]{:S(2)}) collective-permute-start(bf16[8,4,128,128]{3,2,1,0:T(8,128)(2,1)} %get-tuple-element.8.own_hbm), channel_id=1, source_target_pairs={{0,2},{2,4},{4,6},{6,8},{8,10},{10,12},{12,14},{14,0},{1,3},{3,5},... | collective-permute-start | bytes 3145736 | tf_op jit(solution)/shard_map/ppermute | solution.py:427
  22.7 0.7 %copy-start.4 = (f32[8,2]{0,1:T(2,128)S(1)}, f32[8,2]{0,1:T(2,128)}, u32[]{:S(2)}) copy-start(f32[8,2]{0,1:T(2,128)} %param.13) | copy-start | bytes 196
  23.3 1.0 %copy-start.2 = (bf16[8,11,16,128]{3,2,1,0:T(8,128)(2,1)S(1)}, bf16[8,11,16,128]{3,2,1,0:T(8,128)(2,1)}, u32[]{:S(2)}) copy-start(bf16[8,11,16,128]{3,2,1,0:T(8,128)(2,1)} %get-tuple-element.7.blocks_ref) | copy-start | bytes 1081348
  24.3 14.0 %copy-start = (bf16[8,4,128,128]{3,2,1,0:T(8,128)(2,1)S(1)}, bf16[8,4,128,128]{3,2,1,0:T(8,128)(2,1)}, u32[]{:S(2)}) copy-start(bf16[8,4,128,128]{3,2,1,0:T(8,128)(2,1)} %get-tuple-element.8.own_hbm) | copy-start | bytes 3145732
  24.3 14.0 %copy-start.1 = (f32[1,2,128]{2,1,0:T(2,128)S(1)}, f32[1,2,128]{2,1,0:T(2,128)}, u32[]{:S(2)}) copy-start(f32[1,2,128]{2,1,0:T(2,128)} %gain_hbm.1) | copy-start | bytes 3076

commit v4 on v3

v4 whole, which is shorter than its diff:
```python
import math

import jax
import jax.numpy as jnp
from jax import lax
from jax.experimental import pallas as pl
from jax.experimental.pallas import tpu as pltpu
from jax.sharding import PartitionSpec as P

SU = 128
CH = 8
NORM = SU / math.sqrt(128 * 8 * 8 * CH)
SPREAD = 1.5
ROOT = math.sqrt(math.log2(math.e) / (2.0 * SPREAD * SPREAD))
MESH = pl.DeviceIdType.MESH
F32 = jnp.float32
BF16 = jnp.bfloat16
TILES = 11
STEP = 16


def route_kernel(
    vis_hbm, coord_hbm, plane_hbm, group_hbm, raw_hbm, offsets_hbm, centre_hbm, gain_hbm,
    blocks_ref, near_ref, ring_ref, shifted_ref,
    vis_ref, coord_ref, plane_s, group_s, raw_ref, offsets_s, centre_s, gain, constants,
    send, recv, stage, tab, a_send, a_recv, t_send, t_recv, v_send, v_recv, own_sem,
):
    f = lax.axis_index("facet")
    g = lax.axis_index("bl")
    c = lax.axis_index("chan")
    side = (f // 4) * 4
    y = lax.rem(f, 4)
    low = side + lax.rem(y + 3, 4)
    high = side + lax.rem(y + 1, 4)
    far = side + lax.rem(y + 2, 4)

    def flip(facet):
        return lax.rem(facet + 4, 8)

    up, down = (high, g, c), (low, g, c)
    beside, across = (flip(f), g, c), (flip(f), g, 1 - c)
    following = (f, lax.rem(g + 1, 8), c)

    barrier = pltpu.get_barrier_semaphore()
    for d in range(1, 8):
        for peer in ((f, lax.rem(g + d, 8), c), (lax.rem(f + d, 8), g, c)):
            pl.semaphore_signal(barrier, inc=1, device_id=peer, device_id_type=MESH)
    pl.semaphore_signal(barrier, inc=1, device_id=across, device_id_type=MESH)

    fetch_raw = pltpu.make_async_copy(raw_hbm, raw_ref, own_sem.at[2])
    fetch_raw.start()
    names = [
        pltpu.make_async_copy(group_hbm, group_s, own_sem.at[1]),
        pltpu.make_async_copy(plane_hbm, plane_s, own_sem.at[0]),
        pltpu.make_async_copy(vis_hbm, vis_ref, own_sem.at[3]),
        pltpu.make_async_copy(coord_hbm, coord_ref, own_sem.at[4]),
        pltpu.make_async_copy(offsets_hbm, offsets_s, own_sem.at[5]),
        pltpu.make_async_copy(centre_hbm, centre_s, own_sem.at[6]),
        pltpu.make_async_copy(gain_hbm, gain, own_sem.at[7]),
    ]
    for copy in names:
        copy.start()

    wide = (2 * SU, 2 * SU)
    to = lax.broadcasted_iota(jnp.int32, wide, 0)
    source = jnp.where(to < SU, 2 * to, 2 * to - (2 * SU - 1))
    pick = (source == lax.broadcasted_iota(jnp.int32, wide, 1)).astype(F32).astype(BF16)
    fetch_raw.wait()
    first = lax.dot_general(
        raw_ref[0], pick, (((0,), (1,)), ((), ())), preferred_element_type=F32
    ).astype(BF16)
    second = jnp.dot(pick, raw_ref[1], preferred_element_type=F32).astype(BF16)
    tab[0], tab[1] = first[:, :SU], first[:, SU:]
    tab[2], tab[3] = second[:SU], second[SU:]

    for copy in names:
        copy.wait()
    labels = [group_s[n] for n in range(8)]
    rows = lax.broadcasted_iota(jnp.int32, (16, SU), 0)

    def build(group, carry):
        zero = jnp.int32(0)
        i0, i1, n0, n1 = zero, zero, zero, zero
        for n in reversed(range(8)):
            match = labels[n] == group
            i1 = jnp.where(match, i0, i1)
            n1 = jnp.where(match, n0, n1)
            i0 = jnp.where(match, n, i0)
            n0 = jnp.where(match, 1, n0)
        one = vis_ref[i0].astype(F32) * n0.astype(F32)
        two = vis_ref[i1].astype(F32) * n1.astype(F32)
        send[group, 0] = jnp.concatenate([one, two], axis=0).astype(BF16)
        misc = jnp.zeros((16, SU), F32)
        for k, at, here in ((0, i0, n0), (1, i1, n1)):
            spot = coord_ref[at].astype(F32)
            misc = jnp.where(rows == 3 * k, spot[0:1], misc)
            misc = jnp.where(rows == 3 * k + 1, spot[1:2], misc)
            misc = jnp.where(rows == 3 * k + 2, ((plane_s[at] + 1) * here).astype(F32), misc)
        send[group, 1] = misc.astype(BF16)
        return carry

    lax.fori_loop(0, 8, build, 0)

    def line(value):
        return jnp.full((1, SU), value, F32)

    lines = [line(offsets_s[f, k, g].astype(F32)) for k in range(2)]
    for value in (line(centre_s[0, f]), line(centre_s[1, f]), gain[0, 0:1], gain[0, 1:2]):
        for _ in range(3):
            term = value.astype(BF16).astype(F32)
            lines.append(term)
            value = value - term
    lines.append(jnp.zeros((2, SU), F32))
    constants[0] = jnp.concatenate(lines, axis=0).astype(BF16)
    own_constants = pltpu.make_async_copy(constants, blocks_ref.at[pl.ds(88, 1)], own_sem.at[5])
    own_constants.start()
    pl.semaphore_wait(barrier, 15)

    def remote(sems, k, src, dst, peer):
        return pltpu.make_async_remote_copy(
            src_ref=src, dst_ref=dst, send_sem=sems[0].at[k], recv_sem=sems[1].at[k],
            device_id=peer, device_id_type=MESH,
        )

    started = []

    def go(sems, k, src, dst, peer):
        copy = remote(sems, k, src, dst, peer)
        copy.start()
        started.append(copy)

    def landed(sems, k, where):
        remote(sems, k, where, where, up).wait_recv()

    tables, visits = (t_send, t_recv), (v_send, v_recv)

    own_at, flip_at = near_ref.at[0], near_ref.at[1]

    def part(table, half):
        return table.at[pl.ds(2 * half, 2)]

    def sides(half, i):
        return part(ring_ref.at[i], half)

    def block(facet):
        return blocks_ref.at[pl.ds(facet * TILES, TILES)]

    def t_go(k, source, target, peer):
        go(tables, k, source, target, peer)

    def t_landed(k, where):
        landed(tables, k, where)

    for d in range(1, 8):
        peer = lax.rem(g + d, 8)
        copy = pltpu.make_async_remote_copy(
            src_ref=send.at[peer], dst_ref=recv.at[g], send_sem=a_send.at[d],
            recv_sem=a_recv.at[g], device_id=(f, peer, c), device_id_type=MESH,
        )
        copy.start()
        started.append(copy)
    t_go(0, part(tab, 0), sides(0, 0), up)
    t_go(1, part(tab, 1), sides(1, 1), down)
    t_go(2, part(tab, 1), sides(1, 0), up)
    t_go(3, part(tab, 0), sides(0, 1), down)
    t_go(4, part(tab, 0), part(flip_at, 0), beside)
    t_go(5, part(tab, 1), part(flip_at, 1), across)
    t_go(6, tab, shifted_ref.at[0], following)
    own_tab = pltpu.make_async_copy(tab, own_at, own_sem.at[0])
    own_tab.start()
    recv[g] = send[g]
    for d in range(1, 8):
        peer = lax.rem(g + d, 8)
        pltpu.make_async_remote_copy(
            src_ref=send.at[peer], dst_ref=recv.at[peer], send_sem=a_send.at[d],
            recv_sem=a_recv.at[peer], device_id=(f, peer, c), device_id_type=MESH,
        ).wait_recv()

    extra = [jnp.zeros((16, SU), F32) for _ in range(3)]
    for b in range(8):
        stage[b] = recv[b, 0]
        misc = recv[b, 1].astype(F32)
        for k in range(2):
            here = rows == 2 * b + k
            for e in range(3):
                line = 3 * k + e
                extra[e] = jnp.where(here, misc[line : line + 1], extra[e])
    for e in range(3):
        stage[8 + e] = extra[e].astype(BF16)
    peers = (flip(f), high, low, flip(high), flip(low), far, flip(far))
    for k, facet in enumerate(peers):
        go(visits, k, stage, block(f), (facet, g, c))
    own_blocks = pltpu.make_async_copy(stage, block(f), own_sem.at[1])
    own_blocks.start()

    t_landed(0, sides(0, 0))
    t_go(7, sides(0, 0), sides(0, 2), up)
    t_landed(1, sides(1, 1))
    t_go(8, sides(1, 1), sides(1, 2), down)
    t_landed(4, part(flip_at, 0))
    t_landed(5, part(flip_at, 1))
    t_go(9, flip_at, shifted_ref.at[1], following)
    sources = (flip(f), low, high, flip(low), flip(high), far, flip(far))
    for k, facet in enumerate(sources):
        landed(visits, k, block(facet))
    t_landed(2, sides(1, 0))
    t_landed(3, sides(0, 1))
    t_landed(6, shifted_ref.at[0])
    t_landed(7, sides(0, 2))
    t_landed(8, sides(1, 2))
    t_landed(9, shifted_ref.at[1])
    own_constants.wait()
    own_tab.wait()
    own_blocks.wait()
    for copy in started:
        copy.wait_send()


def sine_of_turns(turns):
    part = turns - jnp.floor(turns + 0.5)
    part = jnp.maximum(jnp.minimum(part, 0.5 - part), -0.5 - part)
    angle = part * (2.0 * math.pi)
    square = angle * angle
    total = jnp.full_like(angle, -1.0 / math.factorial(11))
    for power in (9, 7, 5, 3, 1):
        sign = 1.0 if power % 4 == 1 else -1.0
        total = total * square + sign / math.factorial(power)
    return total * angle


def grid_kernel(
    blocks_ref, sums_ref, gains_ref, vis, line_u, line_v, order_v, order, turned, spots, planes, sems,
):
    f = lax.axis_index("facet")
    g = lax.axis_index("bl")
    c = lax.axis_index("chan")
    sub = lax.broadcasted_iota(jnp.int32, (SU, SU), 0)
    lane = lax.broadcasted_iota(jnp.int32, (SU, SU), 1)
    label = jnp.concatenate([blocks_ref[TILES * i + 10] for i in range(8)], axis=0)
    label = label.astype(F32).astype(jnp.int32) - 1
    number = (label >> 3) * 2 + jnp.where((label & 7) == g, 0, 1)
    number = jnp.where(label >= 0, number, 16).astype(F32)
    across = number.T
    ahead = (across < number) | ((across == number) & (lane < sub))
    place = jnp.sum(jnp.where(ahead, 1.0, 0.0), axis=1, keepdims=True)
    hit = place == lane.astype(F32)
    lines = [
        jnp.sum(jnp.where(hit, sub.astype(F32), 0.0), axis=0, keepdims=True),
        jnp.sum(jnp.where(hit, number, 0.0), axis=0, keepdims=True),
        jnp.sum(jnp.where(number < 16.0, 1.0, 0.0), axis=0, keepdims=True),
        jnp.zeros((5, SU), F32),
    ]
    order_v[...] = jnp.concatenate(lines, axis=0).astype(jnp.int32)
    orders = pltpu.make_async_copy(order_v, order, sems.at[0])
    orders.start()

    for i in range(8):
        line_u[16 * i : 16 * i + 16] = blocks_ref[TILES * i + 8].astype(F32)
        line_v[16 * i : 16 * i + 16] = blocks_ref[TILES * i + 9].astype(F32)
        for b in range(8):
            both = blocks_ref[TILES * i + b].astype(F32)
            vis[16 * i + 2 * b] = both[:8]
            vis[16 * i + 2 * b + 1] = both[8:]
    planes[...] = jnp.zeros_like(planes)
    lines = blocks_ref[8 * TILES].astype(F32)
    off_u, off_v = lines[0:1], lines[1:2]
    dir_l, dir_m, gain_u, gain_v = [
        lines[k : k + 1] + lines[k + 1 : k + 2] + lines[k + 2 : k + 3] for k in (2, 5, 8, 11)
    ]
    tall = (64, SU)
    mine = lax.broadcasted_iota(jnp.int32, tall, 1) == lax.broadcasted_iota(jnp.int32, tall, 0) + c * 64
    along_j = jnp.sum(jnp.where(mine, gain_u, 0.0), axis=1, keepdims=True)
    gains_ref[...] = along_j * gain_v * NORM
    orders.wait()
    count = order[2, 0]
    wide = (count + STEP // 2 - 1) // STEP
    narrow = jnp.where(count > wide * STEP, 1, 0)

    row = lax.broadcasted_iota(jnp.int32, (8, SU), 0)
    even = (row & 1) == 0
    channel = (c * 4 + (row >> 1)).astype(F32)
    scale = 1.0 + 0.01 * (channel - 0.5 * (CH - 1))

    def swap(pair):
        return jnp.where(even, pltpu.roll(pair, 7, 0), pltpu.roll(pair, 1, 0))

    def prepare(first, size):
        for q in range(size):
            at = first + q
            slot = order[0, at]
            u = line_u[pl.ds(slot, 1), :]
            v = line_v[pl.ds(slot, 1), :]
            along = jnp.where(even, scale * u - off_u, scale * v - off_v)
            spots[at] = along * ROOT
            turns = (scale * (u * dir_l + v * dir_m)) * (1.0 / SU)
            turns = turns - jnp.floor(turns + 0.5)
            wave = sine_of_turns(turns + jnp.where(even, 0.25, 0.0))
            data = vis[slot]
            straight = data * wave
            crossed = data * swap(wave)
            turned[at] = jnp.where(even, straight - swap(straight), crossed + swap(crossed))

    def every(work):
        def one(step, carry):
            work(step * STEP, STEP)
            return carry

        def rest(step, carry):
            work(wide * STEP, STEP // 2)
            return carry

        lax.fori_loop(0, wide, one, 0)
        lax.fori_loop(0, narrow, rest, 0)

    every(prepare)

    cells = sub.astype(F32) * ROOT

    def profile(line):
        apart = line - cells
        return jnp.exp2(-(apart * apart)).astype(BF16)

    def gather(first, size):
        for q in range(size):
            at = first + q
            along_u, real, imag = [], [], []
            for ch in range(4):
                along_u.append(profile(spots[at, 2 * ch : 2 * ch + 1, :]))
                along_v = profile(spots[at, 2 * ch + 1 : 2 * ch + 2, :])
                for line, parts in ((2 * ch, real), (2 * ch + 1, imag)):
                    weight = jnp.broadcast_to(turned[at, line : line + 1, :], (16, SU)).astype(BF16)
                    parts.append((along_v.reshape(8, 16, SU) * weight[None]).reshape(SU, SU))
            left = jnp.concatenate(along_u, axis=1)
            right = jnp.concatenate(
                [jnp.concatenate(real, axis=1), jnp.concatenate(imag, axis=1)], axis=0
            )
            planes[order[1, at]] += lax.dot_general(
                left, right, (((1,), (1,)), ((), ())), preferred_element_type=F32
            )

    every(gather)
    for p in range(16):
        sums_ref[p] = planes[p].astype(BF16)


def finish_kernel(
    sums_ref, gains_ref, near, ring, shifted, beside, after, both_ways, out_ref, parts, give, came, sems,
):
    f = lax.axis_index("facet")
    g = lax.axis_index("bl")
    c = lax.axis_index("chan")
    partner = (f, g, 1 - c)
    barrier = pltpu.get_barrier_semaphore()
    pl.semaphore_signal(barrier, inc=1, device_id=partner, device_id_type=MESH)
    def turn(re, im):
        return jnp.concatenate(
            [jnp.concatenate([re, im], axis=1), jnp.concatenate([-im, re], axis=1)], axis=0
        )

    side = (f // 4) * 4
    y = lax.rem(f, 4)
    low, high, far = [side + lax.rem(y + d, 4) for d in (3, 1, 2)]

    def flip(facet):
        return lax.rem(facet + 4, 8)

    planes = []
    for shift, ends, round_y, flipped in ((0, near, ring, beside), (1, shifted, after, both_ways)):
        for facet, table in (
            (f, ends.at[0]), (flip(f), ends.at[1]),
            (low, round_y.at[0]), (high, round_y.at[1]), (far, round_y.at[2]),
            (flip(low), flipped.at[0]), (flip(high), flipped.at[1]), (flip(far), flipped.at[2]),
        ):
            planes.append((2 * facet + shift, table))
    for k, (plane, table) in enumerate(planes):
        part = jnp.dot(
            sums_ref[plane], turn(table[2], table[3]), preferred_element_type=F32
        ).astype(BF16)
        parts[k] = turn(part[:, :SU], part[:, SU:])

    def rows_of(half):
        rows = pl.ds(pl.multiple_of(half * 64, 64), 64)
        total = jnp.zeros((64, 2 * SU), F32)
        for k, (_, table) in enumerate(planes):
            both = jnp.concatenate([table[0, rows], table[1, rows]], axis=1)
            total = total + jnp.dot(both, parts[k], preferred_element_type=F32)
        return total

    give[...] = rows_of(1 - c).astype(BF16)
    pl.semaphore_wait(barrier, 1)
    copy = pltpu.make_async_remote_copy(
        src_ref=give, dst_ref=came, send_sem=sems.at[0], recv_sem=sems.at[1],
        device_id=partner, device_id_type=MESH,
    )
    copy.start()
    keep = rows_of(c)
    both = jnp.concatenate([gains_ref[...], gains_ref[...]], axis=1)
    copy.wait()
    out_ref[...] = (keep + came[...].astype(F32)) * both


def body(
    visibilities, coords, plane_index, block_group, offsets, facet_centre, tables, antenna_gain
):
    held = visibilities.shape[0]
    vmem = pl.BlockSpec(memory_space=pltpu.VMEM)
    hbm = pl.BlockSpec(memory_space=pltpu.HBM)
    loose = pl.BlockSpec(memory_space=pl.ANY)
    dma = pltpu.SemaphoreType.DMA
    pair = jax.ShapeDtypeStruct((2, 4, SU, SU), BF16)
    three = jax.ShapeDtypeStruct((3, 4, SU, SU), BF16)
    blocks, near, ring, shifted = pl.pallas_call(
        route_kernel,
        out_shape=(jax.ShapeDtypeStruct((8 * TILES + 1, 16, SU), BF16), pair, three, pair),
        in_specs=[hbm] * 8,
        out_specs=(loose,) * 4,
        scratch_shapes=[
            pltpu.VMEM((held, 8, SU), BF16),
            pltpu.VMEM((held, 2, SU), BF16),
            pltpu.SMEM((held,), jnp.int32),
            pltpu.SMEM((held,), jnp.int32),
            pltpu.VMEM((2, 2 * SU, SU), BF16),
            pltpu.SMEM((8, 2, 8), jnp.int32),
            pltpu.SMEM((2, 8), F32),
            pltpu.VMEM((1, 2, SU), F32),
            pltpu.VMEM((1, 16, SU), BF16),
            pltpu.VMEM((8, 2, 16, SU), BF16),
            pltpu.VMEM((8, 2, 16, SU), BF16),
            pltpu.VMEM((TILES, 16, SU), BF16),
            pltpu.VMEM((4, SU, SU), BF16),
            dma((8,)), dma((8,)), dma((10,)), dma((10,)), dma((7,)), dma((7,)), dma((8,)),
        ],
        compiler_params=pltpu.CompilerParams(
            collective_id=0, has_side_effects=True, vmem_limit_bytes=58 * 2**20
        ),
        name="route",
    )(
        visibilities.reshape(held, 8, SU), coords, plane_index, block_group.reshape(held),
        tables.reshape(2, 2 * SU, SU), offsets.transpose(0, 2, 1), facet_centre.T, antenna_gain,
    )
    axes = ("facet", "bl", "chan")
    devices = [(f, g, c) for f in range(8) for g in range(8) for c in range(2)]

    def number(f, g, c):
        return (f * 8 + g) * 2 + c

    def moved(array, facets, groups, chans):
        pairs = [
            (number(f, g, c), number((f + facets) % 8, (g + groups) % 8, (c + chans) % 2))
            for f, g, c in devices
        ]
        return lax.ppermute(array, axes, pairs)

    others = [moved(ring, *way) for way in ((4, 0, 0), (0, 1, 0), (4, 1, 1))]
    sums, gains = pl.pallas_call(
        grid_kernel,
        out_shape=(
            jax.ShapeDtypeStruct((16, SU, 2 * SU), BF16),
            jax.ShapeDtypeStruct((64, SU), F32),
        ),
        in_specs=[vmem],
        out_specs=(vmem, vmem),
        scratch_shapes=[
            pltpu.VMEM((128, 8, SU), F32),
            pltpu.VMEM((128, SU), F32),
            pltpu.VMEM((128, SU), F32),
            pltpu.VMEM((8, SU), jnp.int32),
            pltpu.SMEM((8, SU), jnp.int32),
            pltpu.VMEM((128, 8, SU), F32),
            pltpu.VMEM((128, 8, SU), F32),
            pltpu.VMEM((17, SU, 2 * SU), F32),
            dma((1,)),
        ],
        compiler_params=pltpu.CompilerParams(vmem_limit_bytes=40 * 2**20),
        cost_estimate=pl.CostEstimate(
            flops=5 * 10**9, bytes_accessed=2 * 10**6, transcendentals=10**7
        ),
        name="grid",
    )(blocks)
    rows_sum = pl.pallas_call(
        finish_kernel,
        out_shape=jax.ShapeDtypeStruct((64, 2 * SU), F32),
        in_specs=[vmem] * 8,
        out_specs=vmem,
        scratch_shapes=[
            pltpu.VMEM((16, 2 * SU, 2 * SU), BF16),
            pltpu.VMEM((64, 2 * SU), BF16),
            pltpu.VMEM((64, 2 * SU), BF16),
            dma((2,)),
        ],
        compiler_params=pltpu.CompilerParams(
            collective_id=1, has_side_effects=True, vmem_limit_bytes=24 * 2**20
        ),
        name="finish",
    )(sums, gains, near, ring, shifted, *others)
    return rows_sum.reshape(1, 1, 64, 2, SU)


def solution(mesh):
    in_specs = (
        P(("facet", "bl"), "chan", None, None),
        P(("facet", "bl"), None, None),
        P(("facet", "bl")),
        P(("facet", "bl"), None),
        P(),
        P(),
        P(("facet", "bl"), None, None, None, None),
        P("bl", None, None),
    )
    out_specs = P("facet", "bl", "chan", None, None)
    return jax.shard_map(body, mesh=mesh, in_specs=in_specs, out_specs=out_specs, check_vma=False)
```

time: 45 us -> 39.9 us (0.89)
  Pallas kernels: 39.6 us -> 35 us
  starting transfers between devices: 0.02 us -> 2.99 us
  waiting for transfers between devices: 2.8 us -> 0.04 us
  local copies, waits for them, and re-layouts: 2.32 us -> 1.66 us
    pallas_call x2, Pallas kernels: 33.8 us -> 29.5 us  [the longest x1 19 us: body(): pl.pallas_call(route_kernel, out_shape=(jax.ShapeDtypeStruct((8 * TILES +...]
    ppermute x1 -> x3, starting transfers between devices: 0.02 us -> 2.99 us  [moved(): return lax.ppermute(array, axes, pairs)]
    ppermute x1 -> x3, waiting for transfers between devices: 2.8 us -> 0.04 us  [moved(): return lax.ppermute(array, axes, pairs)]
    unnamed x10 -> x8, local copies, waits for them, and re-layouts: 1.66 us -> 1 us
  transfers between devices with their start and end apart: 1 -> 3, of which waited for: 1 -> 0; matrix products, arithmetic and copies ran while one was open for 0% -> 0% of each run, Pallas kernels for 25% -> 26%
where the time goes in v4:
time: 39.9 us; the launch traced here: 39.8 us
  Pallas kernels  35 us (88%)
  starting transfers between devices  2.99 us (7%)
  local copies, waits for them, and re-layouts  1.66 us (4%)
    pallas_call x1, Pallas kernels, body(): pl.pallas_call(route_kernel, out_shape=(jax.ShapeDtypeStruct((8 * TILES +...  19 us
    pallas_call x1, Pallas kernels, body(): pl.pallas_call(grid_kernel, out_shape=(jax.ShapeDtypeStruct((16, SU, 2 *...  10.5 us
    pallas_call x1, Pallas kernels, body(): pl.pallas_call(finish_kernel, out_shape=jax.ShapeDtypeStruct((64, 2 * SU)...  5.54 us
    ppermute x3, starting transfers between devices, moved(): return lax.ppermute(array, axes, pairs)  2.99 us
    unnamed x8, local copies, waits for them, and re-layouts  1 us
  transfers between devices with their start and end apart: 3, of which 0 were waited for; matrix products, arithmetic and copies ran while one was open for 0% of the time, Pallas kernels for 26%

profile of v4, /device:TPU:0, one launch (start us, length us, event | category | flops | bytes accessed | tf_op | source)
XLA Modules:
  0.0 39.8 jit_solution(1095149074326369555)
XLA Ops:
  0.0 19.0 %route.1 = (bf16[89,16,128]{2,1,0:T(8,128)(2,1)}, bf16[2,4,128,128]{3,2,1,0:T(8,128)(2,1)}, bf16[3,4,128,128]{3,2,1,0:T(8,128)(2,1)}, bf16[2,4,128,128]{3,2,1,0:T(8,128)(2,1)}) custom-call(bf16[8,8,128]{2,1,0:T(8,128)(2,1)} %bitcast.6, bf16[8,2,128]{2,1,0:T(2,128)(2,1)} %coord_hbm.1, s32[8]{0:T(128)} %plane_hbm.1, s32[8]{0:T(128)} %bitcast.9, ...), custom_call_target="tpu_custom_call" | custom-call | tf_op jit(solution)/shard_map/route/pallas_call | solution.py:412
  19.0 0.4 collective-permute-start
  19.4 0.0 collective-permute-start.1
  19.4 2.6 %collective-permute-start.2 = (bf16[3,4,128,128]{3,2,1,0:T(8,128)(2,1)}, bf16[3,4,128,128]{3,2,1,0:T(8,128)(2,1)S(1)}, u32[]{:S(2)}, u32[]{:S(2)}) collective-permute-start(bf16[3,4,128,128]{3,2,1,0:T(8,128)(2,1)} %get-tuple-element.15.ring), channel_id=1, source_target_pairs={{0,67},{1,66},{2,69},{3,68},{4,71},{5,70},{6,73},{7,72},{8,75},{9,... | collective-permute-start | bytes 1179656 | tf_op jit(solution)/shard_map/ppermute | solution.py:452
  22.0 0.0 copy-start.3
  22.0 1.0 %copy-done.3 = bf16[89,16,128]{2,1,0:T(8,128)(2,1)S(1)} copy-done((bf16[89,16,128]{2,1,0:T(8,128)(2,1)S(1)}, bf16[89,16,128]{2,1,0:T(8,128)(2,1)}, u32[]{:S(2)}) %copy-start.3) | copy-done | bytes 364568
  23.0 0.0 copy-start
  23.0 0.0 copy-start.1
  23.0 0.0 copy-start.2
  23.0 10.5 %grid.1 = (bf16[16,128,256]{2,1,0:T(8,128)(2,1)S(1)}, f32[64,128]{1,0:T(8,128)S(1)}) custom-call(bf16[89,16,128]{2,1,0:T(8,128)(2,1)S(1)} %copy-done.3), custom_call_target="tpu_custom_call" | custom-call | flops 5000000000 | bytes 2000000 | tf_op jit(solution)/shard_map/grid/pallas_call | solution.py:455
  33.5 0.0 collective-permute-done.beside
  33.5 0.0 collective-permute-done.1.after
  33.5 0.0 collective-permute-done.2.both_ways
  33.5 0.0 copy-done
  33.5 0.0 copy-done.1
  33.5 0.0 copy-done.2
  33.5 5.5 %finish.1 = f32[64,256]{1,0:T(8,128)S(1)} custom-call(bf16[16,128,256]{2,1,0:T(8,128)(2,1)S(1)} %get-tuple-element.12.sums_ref, f32[64,128]{1,0:T(8,128)S(1)} %get-tuple-element.13.gains_ref, bf16[2,4,128,128]{3,2,1,0:T(8,128)(2,1)S(1)} %copy-done.1, bf16[3,4,128,128]{3,2,1,0:T(8,128)(2,1)S(1)} %copy-done, bf16[2,4,128,128]{3,2,1,0:T(8,128)(2,1)S(1)} %copy-done.2, ...), custom_call_target="tpu_custom_call" | custom-call | tf_op jit(solution)/shard_map/finish/pallas_call | solution.py:480
  39.1 0.7 %reshape.15 = f32[1,1,64,2,128]{4,3,2,1,0:T(2,128)} reshape(f32[64,256]{1,0:T(8,128)S(1)} %finish.1) | data formatting | bytes 131072 | tf_op jit(solution)/shard_map/reshape | solution.py:496
Async XLA Ops:
  19.0 14.4 %collective-permute-start = (bf16[3,4,128,128]{3,2,1,0:T(8,128)(2,1)}, bf16[3,4,128,128]{3,2,1,0:T(8,128)(2,1)S(1)}, u32[]{:S(2)}, u32[]{:S(2)}) collective-permute-start(bf16[3,4,128,128]{3,2,1,0:T(8,128)(2,1)} %get-tuple-element.15.ring), channel_id=1, source_target_pairs={{0,64},{1,65},{2,66},{3,67},{4,68},{5,69},{6,70},{7,71},{8,72},{9,... | collective-permute-start | bytes 1179656 | tf_op jit(solution)/shard_map/ppermute | solution.py:452
  19.4 14.1 %collective-permute-start.1 = (bf16[3,4,128,128]{3,2,1,0:T(8,128)(2,1)}, bf16[3,4,128,128]{3,2,1,0:T(8,128)(2,1)S(1)}, u32[]{:S(2)}, u32[]{:S(2)}) collective-permute-start(bf16[3,4,128,128]{3,2,1,0:T(8,128)(2,1)} %get-tuple-element.15.ring), channel_id=1, source_target_pairs={{0,2},{1,3},{2,4},{3,5},{4,6},{5,7},{6,8},{7,9},{8,10},{9,11},{10,... | collective-permute-start | bytes 1179656 | tf_op jit(solution)/shard_map/ppermute | solution.py:452
  19.4 14.1 %collective-permute-start.2 = (bf16[3,4,128,128]{3,2,1,0:T(8,128)(2,1)}, bf16[3,4,128,128]{3,2,1,0:T(8,128)(2,1)S(1)}, u32[]{:S(2)}, u32[]{:S(2)}) collective-permute-start(bf16[3,4,128,128]{3,2,1,0:T(8,128)(2,1)} %get-tuple-element.15.ring), channel_id=1, source_target_pairs={{0,67},{1,66},{2,69},{3,68},{4,71},{5,70},{6,73},{7,72},{8,75},{9,... | collective-permute-start | bytes 1179656 | tf_op jit(solution)/shard_map/ppermute | solution.py:452
  22.0 1.0 %copy-start.3 = (bf16[89,16,128]{2,1,0:T(8,128)(2,1)S(1)}, bf16[89,16,128]{2,1,0:T(8,128)(2,1)}, u32[]{:S(2)}) copy-start(bf16[89,16,128]{2,1,0:T(8,128)(2,1)} %get-tuple-element.11.blocks_ref) | copy-start | bytes 1093636
  23.0 10.5 %copy-start = (bf16[3,4,128,128]{3,2,1,0:T(8,128)(2,1)S(1)}, bf16[3,4,128,128]{3,2,1,0:T(8,128)(2,1)}, u32[]{:S(2)}) copy-start(bf16[3,4,128,128]{3,2,1,0:T(8,128)(2,1)} %get-tuple-element.15.ring) | copy-start | bytes 1179652
  23.0 10.5 %copy-start.1 = (bf16[2,4,128,128]{3,2,1,0:T(8,128)(2,1)S(1)}, bf16[2,4,128,128]{3,2,1,0:T(8,128)(2,1)}, u32[]{:S(2)}) copy-start(bf16[2,4,128,128]{3,2,1,0:T(8,128)(2,1)} %get-tuple-element.14.near) | copy-start | bytes 786436
  23.0 10.5 %copy-start.2 = (bf16[2,4,128,128]{3,2,1,0:T(8,128)(2,1)S(1)}, bf16[2,4,128,128]{3,2,1,0:T(8,128)(2,1)}, u32[]{:S(2)}) copy-start(bf16[2,4,128,128]{3,2,1,0:T(8,128)(2,1)} %get-tuple-element.16.shifted) | copy-start | bytes 786436

commit v5 on v4

--- a/solution.py
+++ b/solution.py
@@ -16,7 +16,6 @@
 F32 = jnp.float32
 BF16 = jnp.bfloat16
 TILES = 11
-STEP = 16
 
 
 def route_kernel(
@@ -134,13 +133,13 @@
 
     tables, visits = (t_send, t_recv), (v_send, v_recv)
 
-    own_at, flip_at = near_ref.at[0], near_ref.at[1]
+    own_at, flip_at, low_at, flip_low_at = [near_ref.at[i] for i in range(4)]
 
     def part(table, half):
         return table.at[pl.ds(2 * half, 2)]
 
     def sides(half, i):
-        return part(ring_ref.at[i], half)
+        return part((low_at, ring_ref.at[0], ring_ref.at[1])[i], half)
 
     def block(facet):
         return blocks_ref.at[pl.ds(facet * TILES, TILES)]
@@ -187,7 +186,7 @@
                 extra[e] = jnp.where(here, misc[line : line + 1], extra[e])
     for e in range(3):
         stage[8 + e] = extra[e].astype(BF16)
-    peers = (flip(f), high, low, flip(high), flip(low), far, flip(far))
+    peers = (far, flip(far), flip(high), high, flip(low), low, flip(f))
     for k, facet in enumerate(peers):
         go(visits, k, stage, block(f), (facet, g, c))
     own_blocks = pltpu.make_async_copy(stage, block(f), own_sem.at[1])
@@ -195,20 +194,30 @@
 
     t_landed(0, sides(0, 0))
     t_go(7, sides(0, 0), sides(0, 2), up)
+    t_go(10, part(low_at, 0), part(flip_low_at, 0), across)
     t_landed(1, sides(1, 1))
     t_go(8, sides(1, 1), sides(1, 2), down)
     t_landed(4, part(flip_at, 0))
     t_landed(5, part(flip_at, 1))
     t_go(9, flip_at, shifted_ref.at[1], following)
-    sources = (flip(f), low, high, flip(low), flip(high), far, flip(far))
+    t_landed(2, sides(1, 0))
+    t_go(11, part(low_at, 1), part(flip_low_at, 1), across)
+    t_go(12, low_at, shifted_ref.at[2], following)
+    t_landed(10, part(flip_low_at, 0))
+    t_go(13, part(flip_low_at, 0), part(shifted_ref.at[3], 0), following)
+    t_landed(11, part(flip_low_at, 1))
+    t_go(14, part(flip_low_at, 1), part(shifted_ref.at[3], 1), following)
+    sources = (far, flip(far), flip(low), low, flip(high), high, flip(f))
     for k, facet in enumerate(sources):
         landed(visits, k, block(facet))
-    t_landed(2, sides(1, 0))
     t_landed(3, sides(0, 1))
     t_landed(6, shifted_ref.at[0])
     t_landed(7, sides(0, 2))
     t_landed(8, sides(1, 2))
     t_landed(9, shifted_ref.at[1])
+    t_landed(12, shifted_ref.at[2])
+    t_landed(13, part(shifted_ref.at[3], 0))
+    t_landed(14, part(shifted_ref.at[3], 1))
     own_constants.wait()
     own_tab.wait()
     own_blocks.wait()
@@ -229,7 +238,7 @@
 
 
 def grid_kernel(
-    blocks_ref, sums_ref, gains_ref, vis, line_u, line_v, order_v, order, turned, spots, planes, sems,
+    blocks_ref, planes, gains_ref, vis, line_u, line_v, order_v, order, turned, spots, sems,
 ):
     f = lax.axis_index("facet")
     g = lax.axis_index("bl")
@@ -273,8 +282,7 @@
     gains_ref[...] = along_j * gain_v * NORM
     orders.wait()
     count = order[2, 0]
-    wide = (count + STEP // 2 - 1) // STEP
-    narrow = jnp.where(count > wide * STEP, 1, 0)
+    padded = (count + 3) // 4 * 4
 
     row = lax.broadcasted_iota(jnp.int32, (8, SU), 0)
     even = (row & 1) == 0
@@ -301,16 +309,16 @@
             turned[at] = jnp.where(even, straight - swap(straight), crossed + swap(crossed))
 
     def every(work):
-        def one(step, carry):
-            work(step * STEP, STEP)
-            return carry
-
-        def rest(step, carry):
-            work(wide * STEP, STEP // 2)
-            return carry
-
-        lax.fori_loop(0, wide, one, 0)
-        lax.fori_loop(0, narrow, rest, 0)
+        start = jnp.int32(0)
+        for size in (32, 16, 8, 4):
+            times = padded // 32 if size == 32 else padded // size % 2
+
+            def one(step, carry, start=start, size=size):
+                work(start + step * size, size)
+                return carry
+
+            lax.fori_loop(0, times, one, 0)
+            start = start + times * size
 
     every(prepare)
 
@@ -339,8 +347,6 @@
             )
 
     every(gather)
-    for p in range(16):
-        sums_ref[p] = planes[p].astype(BF16)
 
 
 def finish_kernel(
@@ -367,24 +373,32 @@
     planes = []
     for shift, ends, round_y, flipped in ((0, near, ring, beside), (1, shifted, after, both_ways)):
         for facet, table in (
-            (f, ends.at[0]), (flip(f), ends.at[1]),
-            (low, round_y.at[0]), (high, round_y.at[1]), (far, round_y.at[2]),
-            (flip(low), flipped.at[0]), (flip(high), flipped.at[1]), (flip(far), flipped.at[2]),
+            (f, ends.at[0]), (flip(f), ends.at[1]), (low, ends.at[2]), (flip(low), ends.at[3]),
+            (high, round_y.at[0]), (far, round_y.at[1]),
+            (flip(high), flipped.at[0]), (flip(far), flipped.at[1]),
         ):
             planes.append((2 * facet + shift, table))
     for k, (plane, table) in enumerate(planes):
-        part = jnp.dot(
-            sums_ref[plane], turn(table[2], table[3]), preferred_element_type=F32
+        parts[k] = jnp.dot(
+            sums_ref[plane].astype(BF16), turn(table[2], table[3]), preferred_element_type=F32
         ).astype(BF16)
-        parts[k] = turn(part[:, :SU], part[:, SU:])
 
     def rows_of(half):
         rows = pl.ds(pl.multiple_of(half * 64, 64), 64)
-        total = jnp.zeros((64, 2 * SU), F32)
-        for k, (_, table) in enumerate(planes):
-            both = jnp.concatenate([table[0, rows], table[1, rows]], axis=1)
-            total = total + jnp.dot(both, parts[k], preferred_element_type=F32)
-        return total
+        total = jnp.zeros((SU, 2 * SU), F32)
+        for k in range(0, 16, 2):
+            tall = [
+                jnp.concatenate([table[0, rows], table[1, rows]], axis=0)
+                for _, table in planes[k : k + 2]
+            ]
+            total = total + jnp.dot(
+                jnp.concatenate(tall, axis=1),
+                parts[k : k + 2].reshape(2 * SU, 2 * SU),
+                preferred_element_type=F32,
+            )
+        return jnp.concatenate(
+            [total[:64, :SU] - total[64:, SU:], total[:64, SU:] + total[64:, :SU]], axis=1
+        )
 
     give[...] = rows_of(1 - c).astype(BF16)
     pl.semaphore_wait(barrier, 1)
@@ -407,11 +421,11 @@
     hbm = pl.BlockSpec(memory_space=pltpu.HBM)
     loose = pl.BlockSpec(memory_space=pl.ANY)
     dma = pltpu.SemaphoreType.DMA
-    pair = jax.ShapeDtypeStruct((2, 4, SU, SU), BF16)
-    three = jax.ShapeDtypeStruct((3, 4, SU, SU), BF16)
+    two = jax.ShapeDtypeStruct((2, 4, SU, SU), BF16)
+    four = jax.ShapeDtypeStruct((4, 4, SU, SU), BF16)
     blocks, near, ring, shifted = pl.pallas_call(
         route_kernel,
-        out_shape=(jax.ShapeDtypeStruct((8 * TILES + 1, 16, SU), BF16), pair, three, pair),
+        out_shape=(jax.ShapeDtypeStruct((8 * TILES + 1, 16, SU), BF16), four, two, four),
         in_specs=[hbm] * 8,
         out_specs=(loose,) * 4,
         scratch_shapes=[
@@ -428,7 +442,7 @@
             pltpu.VMEM((8, 2, 16, SU), BF16),
             pltpu.VMEM((TILES, 16, SU), BF16),
             pltpu.VMEM((4, SU, SU), BF16),
-            dma((8,)), dma((8,)), dma((10,)), dma((10,)), dma((7,)), dma((7,)), dma((8,)),
+            dma((8,)), dma((8,)), dma((15,)), dma((15,)), dma((7,)), dma((7,)), dma((8,)),
         ],
         compiler_params=pltpu.CompilerParams(
             collective_id=0, has_side_effects=True, vmem_limit_bytes=58 * 2**20
@@ -455,7 +469,7 @@
     sums, gains = pl.pallas_call(
         grid_kernel,
         out_shape=(
-            jax.ShapeDtypeStruct((16, SU, 2 * SU), BF16),
+            jax.ShapeDtypeStruct((17, SU, 2 * SU), F32),
             jax.ShapeDtypeStruct((64, SU), F32),
         ),
         in_specs=[vmem],
@@ -468,7 +482,6 @@
             pltpu.SMEM((8, SU), jnp.int32),
             pltpu.VMEM((128, 8, SU), F32),
             pltpu.VMEM((128, 8, SU), F32),
-            pltpu.VMEM((17, SU, 2 * SU), F32),
             dma((1,)),
         ],
         compiler_params=pltpu.CompilerParams(vmem_limit_bytes=40 * 2**20),
@@ -483,7 +496,7 @@
         in_specs=[vmem] * 8,
         out_specs=vmem,
         scratch_shapes=[
-            pltpu.VMEM((16, 2 * SU, 2 * SU), BF16),
+            pltpu.VMEM((16, SU, 2 * SU), BF16),
             pltpu.VMEM((64, 2 * SU), BF16),
             pltpu.VMEM((64, 2 * SU), BF16),
             dma((2,)),

time: 39.9 us -> 38.6 us (0.967)
  Pallas kernels: 35 us -> 33.3 us
    pallas_call x1, Pallas kernels: 10.5 us -> 8.86 us  [body(): pl.pallas_call(grid_kernel, out_shape=(jax.ShapeDtypeStruct((17, SU, 2 *...]
  transfers between devices with their start and end apart: 3 -> 3, of which waited for: 0 -> 0; matrix products, arithmetic and copies ran while one was open for 0% -> 0% of each run, Pallas kernels for 26% -> 23%
where the time goes in v5:
time: 38.6 us; the launch traced here: 38.3 us
  Pallas kernels  33.3 us (86%)
  starting transfers between devices  3.24 us (8%)
  local copies, waits for them, and re-layouts  1.66 us (4%)
    pallas_call x1, Pallas kernels, body(): pl.pallas_call(route_kernel, out_shape=(jax.ShapeDtypeStruct((8 * TILES +...  18.9 us
    pallas_call x1, Pallas kernels, body(): pl.pallas_call(grid_kernel, out_shape=(jax.ShapeDtypeStruct((17, SU, 2 *...  8.86 us
    pallas_call x1, Pallas kernels, body(): pl.pallas_call(finish_kernel, out_shape=jax.ShapeDtypeStruct((64, 2 * SU)...  5.54 us
    ppermute x3, starting transfers between devices, moved(): return lax.ppermute(array, axes, pairs)  3.24 us
    unnamed x8, local copies, waits for them, and re-layouts  1 us
  transfers between devices with their start and end apart: 3, of which 0 were waited for; matrix products, arithmetic and copies ran while one was open for 0% of the time, Pallas kernels for 23%

profile of v5, /device:TPU:0, one launch (start us, length us, event | category | flops | bytes accessed | tf_op | source)
XLA Modules:
  0.0 38.3 jit_solution(3364483410006198858)
XLA Ops:
  0.0 18.9 %route.1 = (bf16[89,16,128]{2,1,0:T(8,128)(2,1)}, bf16[4,4,128,128]{3,2,1,0:T(8,128)(2,1)}, bf16[2,4,128,128]{3,2,1,0:T(8,128)(2,1)}, bf16[4,4,128,128]{3,2,1,0:T(8,128)(2,1)}) custom-call(bf16[8,8,128]{2,1,0:T(8,128)(2,1)} %bitcast.6, bf16[8,2,128]{2,1,0:T(2,128)(2,1)} %coord_hbm.1, s32[8]{0:T(128)} %plane_hbm.1, s32[8]{0:T(128)} %bitcast.9, ...), custom_call_target="tpu_custom_call" | custom-call | tf_op jit(solution)/shard_map/route/pallas_call | solution.py:426
  18.9 0.5 %collective-permute-start = (bf16[2,4,128,128]{3,2,1,0:T(8,128)(2,1)}, bf16[2,4,128,128]{3,2,1,0:T(8,128)(2,1)S(1)}, u32[]{:S(2)}, u32[]{:S(2)}) collective-permute-start(bf16[2,4,128,128]{3,2,1,0:T(8,128)(2,1)} %get-tuple-element.15.ring), channel_id=1, source_target_pairs={{0,64},{1,65},{2,66},{3,67},{4,68},{5,69},{6,70},{7,71},{8,72},{9,... | collective-permute-start | bytes 786440 | tf_op jit(solution)/shard_map/ppermute | solution.py:466
  19.4 0.0 collective-permute-start.1
  19.4 2.8 %collective-permute-start.2 = (bf16[2,4,128,128]{3,2,1,0:T(8,128)(2,1)}, bf16[2,4,128,128]{3,2,1,0:T(8,128)(2,1)S(1)}, u32[]{:S(2)}, u32[]{:S(2)}) collective-permute-start(bf16[2,4,128,128]{3,2,1,0:T(8,128)(2,1)} %get-tuple-element.15.ring), channel_id=1, source_target_pairs={{0,67},{1,66},{2,69},{3,68},{4,71},{5,70},{6,73},{7,72},{8,75},{9,... | collective-permute-start | bytes 786440 | tf_op jit(solution)/shard_map/ppermute | solution.py:466
  22.1 0.0 copy-start.3
  22.1 1.0 %copy-done.3 = bf16[89,16,128]{2,1,0:T(8,128)(2,1)S(1)} copy-done((bf16[89,16,128]{2,1,0:T(8,128)(2,1)S(1)}, bf16[89,16,128]{2,1,0:T(8,128)(2,1)}, u32[]{:S(2)}) %copy-start.3) | copy-done | bytes 364568
  23.1 0.0 copy-start
  23.1 0.0 copy-start.1
  23.1 0.0 copy-start.2
  23.1 8.9 %grid.1 = (f32[17,128,256]{2,1,0:T(8,128)S(1)}, f32[64,128]{1,0:T(8,128)S(1)}) custom-call(bf16[89,16,128]{2,1,0:T(8,128)(2,1)S(1)} %copy-done.3), custom_call_target="tpu_custom_call" | custom-call | flops 5000000000 | bytes 2000000 | tf_op jit(solution)/shard_map/grid/pallas_call | solution.py:469
  32.0 0.0 collective-permute-done.beside
  32.0 0.0 collective-permute-done.1.after
  32.0 0.0 collective-permute-done.2.both_ways
  32.0 0.0 copy-done
  32.0 0.0 copy-done.1
  32.1 0.0 copy-done.2
  32.1 5.5 %finish.1 = f32[64,256]{1,0:T(8,128)S(1)} custom-call(f32[17,128,256]{2,1,0:T(8,128)S(1)} %get-tuple-element.12.sums_ref, f32[64,128]{1,0:T(8,128)S(1)} %get-tuple-element.13.gains_ref, bf16[4,4,128,128]{3,2,1,0:T(8,128)(2,1)S(1)} %copy-done, bf16[2,4,128,128]{3,2,1,0:T(8,128)(2,1)S(1)} %copy-done.2, bf16[4,4,128,128]{3,2,1,0:T(8,128)(2,1)S(1)} %copy-done.1, ...), custom_call_target="tpu_custom_call" | custom-call | tf_op jit(solution)/shard_map/finish/pallas_call | solution.py:493
  37.6 0.7 %reshape.15 = f32[1,1,64,2,128]{4,3,2,1,0:T(2,128)} reshape(f32[64,256]{1,0:T(8,128)S(1)} %finish.1) | data formatting | bytes 131072 | tf_op jit(solution)/shard_map/reshape | solution.py:509
Async XLA Ops:
  18.9 13.1 %collective-permute-start = (bf16[2,4,128,128]{3,2,1,0:T(8,128)(2,1)}, bf16[2,4,128,128]{3,2,1,0:T(8,128)(2,1)S(1)}, u32[]{:S(2)}, u32[]{:S(2)}) collective-permute-start(bf16[2,4,128,128]{3,2,1,0:T(8,128)(2,1)} %get-tuple-element.15.ring), channel_id=1, source_target_pairs={{0,64},{1,65},{2,66},{3,67},{4,68},{5,69},{6,70},{7,71},{8,72},{9,... | collective-permute-start | bytes 786440 | tf_op jit(solution)/shard_map/ppermute | solution.py:466
  19.4 12.6 %collective-permute-start.1 = (bf16[2,4,128,128]{3,2,1,0:T(8,128)(2,1)}, bf16[2,4,128,128]{3,2,1,0:T(8,128)(2,1)S(1)}, u32[]{:S(2)}, u32[]{:S(2)}) collective-permute-start(bf16[2,4,128,128]{3,2,1,0:T(8,128)(2,1)} %get-tuple-element.15.ring), channel_id=1, source_target_pairs={{0,2},{1,3},{2,4},{3,5},{4,6},{5,7},{6,8},{7,9},{8,10},{9,11},{10,... | collective-permute-start | bytes 786440 | tf_op jit(solution)/shard_map/ppermute | solution.py:466
  19.4 12.6 %collective-permute-start.2 = (bf16[2,4,128,128]{3,2,1,0:T(8,128)(2,1)}, bf16[2,4,128,128]{3,2,1,0:T(8,128)(2,1)S(1)}, u32[]{:S(2)}, u32[]{:S(2)}) collective-permute-start(bf16[2,4,128,128]{3,2,1,0:T(8,128)(2,1)} %get-tuple-element.15.ring), channel_id=1, source_target_pairs={{0,67},{1,66},{2,69},{3,68},{4,71},{5,70},{6,73},{7,72},{8,75},{9,... | collective-permute-start | bytes 786440 | tf_op jit(solution)/shard_map/ppermute | solution.py:466
  22.1 1.0 %copy-start.3 = (bf16[89,16,128]{2,1,0:T(8,128)(2,1)S(1)}, bf16[89,16,128]{2,1,0:T(8,128)(2,1)}, u32[]{:S(2)}) copy-start(bf16[89,16,128]{2,1,0:T(8,128)(2,1)} %get-tuple-element.11.blocks_ref) | copy-start | bytes 1093636
  23.1 8.9 %copy-start = (bf16[4,4,128,128]{3,2,1,0:T(8,128)(2,1)S(1)}, bf16[4,4,128,128]{3,2,1,0:T(8,128)(2,1)}, u32[]{:S(2)}) copy-start(bf16[4,4,128,128]{3,2,1,0:T(8,128)(2,1)} %get-tuple-element.14.near) | copy-start | bytes 1572868
  23.1 8.9 %copy-start.1 = (bf16[4,4,128,128]{3,2,1,0:T(8,128)(2,1)S(1)}, bf16[4,4,128,128]{3,2,1,0:T(8,128)(2,1)}, u32[]{:S(2)}) copy-start(bf16[4,4,128,128]{3,2,1,0:T(8,128)(2,1)} %get-tuple-element.16.shifted) | copy-start | bytes 1572868
  23.1 8.9 %copy-start.2 = (bf16[2,4,128,128]{3,2,1,0:T(8,128)(2,1)S(1)}, bf16[2,4,128,128]{3,2,1,0:T(8,128)(2,1)}, u32[]{:S(2)}) copy-start(bf16[2,4,128,128]{3,2,1,0:T(8,128)(2,1)} %get-tuple-element.15.ring) | copy-start | bytes 786436
